TPU v7x, 32 devices: a whole 2x2x4 slice. The times are simulated.
32 devices in a mesh: groups: 2 (over x), seq: 16 (over z, y, core).
Axes of the slice: x: 2, y: 2, z: 4, core: 2. Of those that a mesh axis runs over, the one named last changes fastest.
Arguments:
- frames_in: bfloat16 [4096, 1024], P(('groups', 'seq')), parts along dimension 0, may hold values from -6 to 6
- query_proj: bfloat16 [4096, 512], P(('groups', 'seq')), parts along dimension 0, may hold values from -6 to 6
- key_proj: bfloat16 [4096, 512], P(('groups', 'seq')), parts along dimension 0, may hold values from -6 to 6
- value_proj: bfloat16 [4096, 512], P(('groups', 'seq')), parts along dimension 0, may hold values from -6 to 6
- utterance_lengths: int32 [32], P('groups'), parts along dimension 0, may hold values from 1 to 256, 2048 in all
- bucket_table: int32 [767], replicated, may hold values from 0 to 31
- bucket_bias: float32 [32, 8], replicated, may hold values from -4 to 4
- out_weight: bfloat16 [512, 1024], replicated, may hold values from -0.25 to 0.25
- norm_gain: float32 [1024], replicated, may hold values from 0.1 to 1.9
- expand_weight: bfloat16 [1024, 2048], replicated, may hold values from -0.1875 to 0.1875
- depth_taps: float32 [31, 1024], replicated, may hold values from -1 to 1
- inner_gain: float32 [1024], replicated, may hold values from 0.1 to 1.9
- shrink_weight: bfloat16 [1024, 1024], replicated, may hold values from -0.1875 to 0.1875
Outputs:
- block_out: bfloat16 [4096, 1024], P(('groups', 'seq')), parts along dimension 0
There are 2 independent parts, one for each index of `groups`. A program takes and returns all parts, laid end to end along the dimension named above; an argument that names none is the same for every part. Nothing has to cross between parts.
Inputs may be any that keep to these rules, and one draw needn't show every extreme that they name: `utterance_lengths`: they sum to 2048, and one is exactly 256.
All inputs are finite; a program needn't handle non-finite values.
Results may differ from a plain program's by a relative error of at most 0.014.
Values may be sent and summed in bfloat16 or wider, within the bound.
A program may use at most 64 MiB of HBM per device.

v0:
```python
import jax
import jax.numpy as jnp
from jax import lax
from jax.sharding import PartitionSpec as P

KERNEL = 31
DILATION = 4
REACH = 2


norm_epsilon = 1e-05
masked_score = -1e30


def shifted(value, axis, steps):
    count = lax.axis_size(axis)
    leading, last = (max(0, -steps), min(count, count - steps))
    return lax.ppermute(value, axis, [(source, source + steps) for source in range(leading, last)])


def padded_2(cells, sides, width):
    for axis, dim in sides:
        count = lax.axis_size(axis)
        ends = count - 1
        head = lax.slice_in_dim(cells, 0, width, axis=dim)
        tail = lax.slice_in_dim(cells, cells.shape[dim] - width, cells.shape[dim], axis=dim)
        cells = jnp.concatenate(
            [
                lax.ppermute(tail, axis, [(i, (i + 1) % count) for i in range(ends)]),
                cells,
                lax.ppermute(head, axis, [((i + 1) % count, i) for i in range(ends)]),
            ],
            axis=dim,
        )
    return cells


def segment_of(positions, bounds):
    inside = jnp.sum((positions[:, None] >= bounds[None, :]).astype(jnp.int32), axis=1)
    return jnp.where(positions < 0, -1, inside)


def layer_norm(values, gain_vec):
    row_mean = jnp.mean(values, axis=-1, keepdims=True)
    centred = values - row_mean
    spread = jnp.mean(centred * centred, axis=-1, keepdims=True)
    return centred * lax.rsqrt(spread + norm_epsilon) * gain_vec


def gated_units(mid, norm_gain, expand_weight):
    model_width = mid.shape[1]
    normed = layer_norm(mid.astype(jnp.float32), norm_gain).astype(jnp.bfloat16)
    hidden = jnp.dot(normed, expand_weight, preferred_element_type=jnp.float32)
    return (hidden[:, :model_width] * jax.nn.sigmoid(hidden[:, model_width:])).astype(jnp.bfloat16)


def on_device(
    frames_in,
    query_proj,
    key_proj,
    value_proj,
    utterance_lengths,
    bucket_table,
    bucket_bias,
    out_weight,
    norm_gain,
    expand_weight,
    depth_taps,
    inner_gain,
    shrink_weight,
):
    row_count = query_proj.shape[0]
    head_count = bucket_bias.shape[1]
    att_width = query_proj.shape[1]
    head_width = att_width // head_count
    model_width = frames_in.shape[1]
    line_length = bucket_table.shape[0]
    window_cols = (2 * REACH + 1) * row_count
    device_index = lax.axis_index("seq")
    bounds = jnp.cumsum(utterance_lengths)
    offsets = jnp.arange(row_count, dtype=jnp.int32)
    query_segment = segment_of(device_index * row_count + offsets, bounds)
    bucket_hits = (
        bucket_table[:, None] == jnp.arange(bucket_bias.shape[0], dtype=jnp.int32)[None, :]
    ).astype(jnp.float32)
    bias_line = jnp.dot(bucket_hits, bucket_bias, precision=lax.Precision.HIGHEST).T
    repeated = jnp.tile(bias_line, (1, row_count + 1))
    skewed = repeated[:, row_count - 1 : row_count - 1 + row_count * (line_length - 1)]
    window_bias = skewed.reshape(head_count, row_count, line_length - 1)[:, :, :window_cols]
    queries = query_proj.reshape(row_count, head_count, head_width).transpose(1, 0, 2)
    scaling = head_width ** (-0.5)

    def absorb(state, packed_block, hop_count, key_segment):
        run_max, run_total, run_acc = state
        keys_here = packed_block[:, :att_width].reshape(row_count, head_count, head_width)
        values_here = packed_block[:, att_width:].reshape(row_count, head_count, head_width)
        scores = jnp.einsum("hrd,chd->hrc", queries, keys_here, preferred_element_type=jnp.float32)
        first_col = (hop_count + REACH) * row_count
        scores = scores * scaling + window_bias[:, :, first_col : first_col + row_count]
        same_utterance = (query_segment[:, None] == key_segment[None, :])[None]
        scores = jnp.where(same_utterance, scores, masked_score)
        new_max = jnp.maximum(run_max, jnp.max(scores, axis=2))
        weights = jnp.exp(scores - new_max[:, :, None])
        rescale = jnp.exp(run_max - new_max)
        new_total = run_total * rescale + jnp.sum(weights, axis=2)
        weighted = jnp.einsum(
            "hrc,chd->hrd",
            weights.astype(jnp.bfloat16),
            values_here,
            preferred_element_type=jnp.float32,
        )
        return (new_max, new_total, run_acc * rescale[:, :, None] + weighted)

    def visit(state, packed_block, hop_count):
        key_segment = segment_of((device_index + hop_count) * row_count + offsets, bounds)
        return absorb(state, packed_block, hop_count, key_segment)

    packed = jnp.concatenate([key_proj, value_proj], axis=1)
    state = (
        jnp.full((head_count, row_count), masked_score, jnp.float32),
        jnp.zeros((head_count, row_count), jnp.float32),
        jnp.zeros((head_count, row_count, head_width), jnp.float32),
    )
    state = visit(state, packed, 0)
    from_next = packed
    from_prev = packed
    for hop_count in range(1, REACH + 1):
        from_next = shifted(from_next, "seq", -1)
        from_prev = shifted(from_prev, "seq", 1)
        state = visit(state, from_next, hop_count)
        state = visit(state, from_prev, -hop_count)
    run_max, run_total, run_acc = state
    attended = (
        (run_acc / run_total[:, :, None])
        .astype(jnp.bfloat16)
        .transpose(1, 0, 2)
        .reshape(row_count, att_width)
    )
    mid = (
        frames_in.astype(jnp.float32)
        + jnp.dot(attended, out_weight, preferred_element_type=jnp.float32)
    ).astype(jnp.bfloat16)
    halo_rows = DILATION * (KERNEL - 1) // 2
    gated = gated_units(mid, norm_gain, expand_weight)
    padded = padded_2(gated, (("seq", 0),), halo_rows)
    phased = padded.reshape(-1, DILATION, model_width)
    step_rows = row_count // DILATION
    conv_sum = jnp.zeros((step_rows, DILATION, model_width), jnp.float32)
    for tap_index in range(KERNEL):
        conv_sum = conv_sum + depth_taps[tap_index] * phased[
            tap_index : tap_index + step_rows
        ].astype(jnp.float32)
    conv_sum = conv_sum.reshape(row_count, model_width)
    inner_normed = layer_norm(conv_sum, inner_gain)
    activated = (inner_normed * jax.nn.sigmoid(inner_normed)).astype(jnp.bfloat16)
    return (
        mid.astype(jnp.float32)
        + jnp.dot(activated, shrink_weight, preferred_element_type=jnp.float32)
    ).astype(jnp.bfloat16)


def solution(mesh):
    placed = (
        P(("groups", "seq"), None),
        P(("groups", "seq"), None),
        P(("groups", "seq"), None),
        P(("groups", "seq"), None),
        P("groups"),
        P(),
        P(),
        P(),
        P(),
        P(),
        P(),
        P(),
        P(),
    )
    return jax.shard_map(
        on_device, mesh=mesh, in_specs=placed, out_specs=P(("groups", "seq"), None), check_vma=False
    )
```

profile of v0, /device:TPU:21, one launch (start us, length us, event | category | flops | bytes accessed | tf_op | source)
XLA Modules:
  0.0 97.3 jit_solution(1213232763662413313)
XLA Ops:
  0.0 1.7 %constant_dynamic-update-slice_fusion.1 = bf16[128,1024]{1,0:T(8,128)(2,1)} fusion(bf16[128,512]{1,0:T(8,128)(2,1)} %param.15), kind=kLoop, calls=%fused_computation.179 | loop fusion | bytes 262144
  1.7 1.6 %constant_dynamic-update-slice_fusion = bf16[128,1024]{1,0:T(8,128)(2,1)} fusion(bf16[128,1024]{1,0:T(8,128)(2,1)} %constant_dynamic-update-slice_fusion.1, bf16[128,512]{1,0:T(8,128)(2,1)} %param.16), kind=kLoop, calls=%fused_computation.178 | loop fusion | bytes 262144 | tf_op jit(solution)/shard_map/concatenate | solution.py:118
  3.3 3.7 %collective-permute-start.1 = (bf16[128,1024]{1,0:T(8,128)(2,1)}, bf16[128,1024]{1,0:T(8,128)(2,1)}, u32[]{:S(2)}, u32[]{:S(2)}) collective-permute-start(bf16[128,1024]{1,0:T(8,128)(2,1)} %constant_dynamic-update-slice_fusion), channel_id=1, source_target_pairs={{0,1},{1,2},{2,3},{3,4},{4,5},{5,6},{6,7},{7,8},{8,9},{9,10},{10,1... | collective-permute-start | bytes 786440 | tf_op jit(solution)/shard_map/ppermute | solution.py:18
  7.0 1.9 %collective-permute-start = (bf16[128,1024]{1,0:T(8,128)(2,1)}, bf16[128,1024]{1,0:T(8,128)(2,1)}, u32[]{:S(2)}, u32[]{:S(2)}) collective-permute-start(bf16[128,1024]{1,0:T(8,128)(2,1)} %constant_dynamic-update-slice_fusion), channel_id=1, source_target_pairs={{1,0},{2,1},{3,2},{4,3},{5,4},{6,5},{7,6},{8,7},{9,8},{10,9},{11,1... | collective-permute-start | bytes 786440 | tf_op jit(solution)/shard_map/ppermute | solution.py:18
  9.0 0.7 copy.55
  9.8 0.1 reduce
  9.9 0.1 convert_reduce_fusion
  10.0 0.6 compare_select_fusion.4
  10.6 1.1 %convolution_bitcast_fusion.5 = f32[8,767]{1,0:T(8,128)S(1)} fusion(f32[32,8]{0,1:T(8,128)} %param.19, s32[767]{0:T(1024)} %param.18), kind=kOutput, calls=%fused_computation.68 | convolution fusion | flops 2380768 | bytes 28636 | tf_op jit(solution)/shard_map/dot_general | solution.py:86
  11.6 2.0 %tile.4 = f32[8,129,767]{2,1,0:T(8,128)} broadcast(f32[8,767]{1,0:T(8,128)S(1)} %convolution_bitcast_fusion.5), dimensions={0,2} | broadcast | bytes 3190720 | tf_op jit(solution)/shard_map/tile | solution.py:87
  13.6 4.7 %tile.10 = f32[8,98943]{1,0:T(8,128)} reshape(f32[8,129,767]{2,1,0:T(8,128)} %tile.4) | data formatting | bytes 6332352 | tf_op jit(solution)/shard_map/tile | solution.py:87
  18.3 4.5 %slice.384 = f32[8,98048]{1,0:T(8,128)} slice(f32[8,98943]{1,0:T(8,128)} %tile.10), slice={[0:8], [127:98175]} | slice | bytes 6275072 | tf_op jit(solution)/shard_map/slice | solution.py:88
  22.7 7.0 %reshape.468 = f32[8,128,766]{2,1,0:T(8,128)} reshape(f32[8,98048]{1,0:T(8,128)} %slice.384) | data formatting | bytes 6275072 | tf_op jit(solution)/shard_map/reshape | solution.py:89
  29.7 3.0 %fusion.104 = (f32[8,128,128]{2,1,0:T(8,128)}, f32[8,128,128]{2,1,0:T(8,128)}, f32[8,128,128]{2,1,0:T(8,128)S(1)}, f32[8,128,128]{2,1,0:T(8,128)S(1)}, f32[8,128,128]{2,1,0:T(8,128)}) fusion(f32[8,128,766]{2,1,0:T(8,128)} %reshape.468), kind=kLoop, calls=%fused_computation.220 | loop fusion | bytes 5242880 | tf_op jit(solution)/shard_map/slice | solution.py:99
  32.7 0.7 fusion.110
  33.4 0.8 broadcast_compare_fusion.2
  34.2 0.8 copy.57
  35.0 0.1 copy.60
  35.1 2.1 %copy.87 = f32[8,128,128]{1,2,0:T(8,128)} copy(f32[8,128,128]{2,1,0:T(8,128)} %get-tuple-element.24) | data formatting | bytes 1048576
  37.2 1.0 %copy.56 = bf16[128,512]{0,1:T(8,128)(2,1)S(1)} copy(bf16[128,512]{1,0:T(8,128)(2,1)} %param.14) | data formatting | bytes 262144 | tf_op args[1]
  38.2 2.0 %copy.86 = f32[8,128,128]{1,2,0:T(8,128)} copy(f32[8,128,128]{2,1,0:T(8,128)} %get-tuple-element.21) | data formatting | bytes 1048576
  40.2 2.0 %copy.85 = f32[8,128,128]{1,2,0:T(8,128)} copy(f32[8,128,128]{2,1,0:T(8,128)} %get-tuple-element.20) | data formatting | bytes 1048576
  42.3 1.0 %copy.84 = f32[8,128,128]{1,2,0:T(8,128)} copy(f32[8,128,128]{2,1,0:T(8,128)S(1)} %get-tuple-element.22) | data formatting | bytes 1048576
  43.3 0.2 copy.83
  43.5 1.6 %fusion.116 = (f32[8,128]{1,0:T(8,128)}, f32[8,128,128]{1,2,0:T(8,128)S(1)}) fusion(f32[8,128,128]{1,2,0:T(8,128)S(1)} %copy.83, bf16[8,128,64]{1,2,0:T(8,128)(2,1)S(1)} %bitcast.220, bf16[128,8,64]{0,2,1:T(8,128)(2,1)S(1)} %bitcast.231, pred[128,128]{0,1:T(8,128)(4,1)} %get-tuple-element.73), kind=kOutput, calls=%fused_computation.232 | convolution fusion | flops 17300480 | bytes 1331200 | tf_op jit(solution)/shard_map/hrd,chd->hrc/dot_general | solution.py:97
  45.1 1.6 %fusion.108 = (bf16[128,512]{1,0:T(8,128)(2,1)}, bf16[128,512]{1,0:T(8,128)(2,1)S(1)}) fusion(bf16[128,1024]{1,0:T(8,128)(2,1)} %collective-permute-done.1), kind=kLoop, calls=%fused_computation.224 | loop fusion | bytes 524288 | tf_op jit(solution)/shard_map/slice | solution.py:96
  46.8 0.1 copy.66
  46.9 4.5 %collective-permute-start.3 = (bf16[128,1024]{1,0:T(8,128)(2,1)}, bf16[128,1024]{1,0:T(8,128)(2,1)}, u32[]{:S(2)}, u32[]{:S(2)}) collective-permute-start(bf16[128,1024]{1,0:T(8,128)(2,1)} %collective-permute-done.1), channel_id=1, source_target_pairs={{0,1},{1,2},{2,3},{3,4},{4,5},{5,6},{6,7},{7,8},{8,9},{9,10},{10,1... | collective-permute-start | bytes 786440 | tf_op jit(solution)/shard_map/ppermute | solution.py:18
  51.4 1.9 %fusion.114 = (f32[8,128]{1,0:T(8,128)}, f32[8,128,128]{1,2,0:T(8,128)S(1)}) fusion(f32[8,128,128]{1,2,0:T(8,128)} %copy.85, bf16[128,8,64]{0,2,1:T(8,128)(2,1)S(1)} %bitcast.232, bf16[8,128,64]{1,2,0:T(8,128)(2,1)S(1)} %bitcast.221, pred[128,128]{0,1:T(8,128)(4,1)} %get-tuple-element.69), kind=kOutput, calls=%fused_computation.230 | convolution fusion | flops 17300480 | bytes 1331200 | tf_op jit(solution)/shard_map/hrd,chd->hrc/dot_general | solution.py:97
  53.4 1.6 %fusion.109 = (bf16[128,512]{1,0:T(8,128)(2,1)S(1)}, bf16[128,512]{1,0:T(8,128)(2,1)}) fusion(bf16[128,1024]{1,0:T(8,128)(2,1)} %collective-permute-done), kind=kLoop, calls=%fused_computation.225 | loop fusion | bytes 524288 | tf_op jit(solution)/shard_map/slice | solution.py:96
  55.0 1.7 %copy.62 = bf16[128,512]{0,1:T(8,128)(2,1)} copy(bf16[128,512]{1,0:T(8,128)(2,1)} %get-tuple-element.34) | data formatting | bytes 262144 | tf_op jit(solution)/shard_map/slice | solution.py:95
  56.7 1.9 %collective-permute-start.2 = (bf16[128,1024]{1,0:T(8,128)(2,1)}, bf16[128,1024]{1,0:T(8,128)(2,1)}, u32[]{:S(2)}, u32[]{:S(2)}) collective-permute-start(bf16[128,1024]{1,0:T(8,128)(2,1)} %collective-permute-done), channel_id=1, source_target_pairs={{1,0},{2,1},{3,2},{4,3},{5,4},{6,5},{7,6},{8,7},{9,8},{10,9},{11,1... | collective-permute-start | bytes 786440 | tf_op jit(solution)/shard_map/ppermute | solution.py:18
  58.6 2.8 %fusion.115 = (f32[8,128]{1,0:T(8,128)}, f32[8,128,128]{1,2,0:T(8,128)}) fusion(f32[8,128,128]{1,2,0:T(8,128)} %copy.84, bf16[128,8,64]{0,2,1:T(8,128)(2,1)} %bitcast.233, bf16[8,128,64]{1,2,0:T(8,128)(2,1)S(1)} %bitcast.222, pred[128,128]{0,1:T(8,128)(4,1)} %get-tuple-element.72), kind=kOutput, calls=%fused_computation.231 | convolution fusion | flops 17300480 | bytes 1331200 | tf_op jit(solution)/shard_map/hrd,chd->hrc/dot_general | solution.py:97
  61.4 0.8 copy.64
  62.1 1.0 %copy.68 = bf16[128,512]{0,1:T(8,128)(2,1)S(1)} copy(bf16[128,512]{1,0:T(8,128)(2,1)} %get-tuple-element.31) | data formatting | bytes 262144 | tf_op jit(solution)/shard_map/slice | solution.py:96
  63.2 1.7 %fusion.106 = (bf16[128,512]{1,0:T(8,128)(2,1)}, bf16[128,512]{1,0:T(8,128)(2,1)}) fusion(bf16[128,1024]{1,0:T(8,128)(2,1)} %collective-permute-done.3), kind=kLoop, calls=%fused_computation.222 | loop fusion | bytes 524288 | tf_op jit(solution)/shard_map/slice | solution.py:96
  64.9 1.7 %copy.74 = bf16[128,512]{0,1:T(8,128)(2,1)} copy(bf16[128,512]{1,0:T(8,128)(2,1)} %get-tuple-element.28) | data formatting | bytes 262144 | tf_op jit(solution)/shard_map/slice | solution.py:95
  66.5 1.7 %fusion.107 = (bf16[128,512]{1,0:T(8,128)(2,1)}, bf16[128,512]{1,0:T(8,128)(2,1)}) fusion(bf16[128,1024]{1,0:T(8,128)(2,1)} %collective-permute-done.2), kind=kLoop, calls=%fused_computation.223 | loop fusion | bytes 524288 | tf_op jit(solution)/shard_map/slice | solution.py:96
  68.2 1.7 %copy.70 = bf16[128,512]{0,1:T(8,128)(2,1)} copy(bf16[128,512]{1,0:T(8,128)(2,1)} %get-tuple-element.30) | data formatting | bytes 262144 | tf_op jit(solution)/shard_map/slice | solution.py:95
  69.9 1.7 %copy.72 = bf16[128,512]{0,1:T(8,128)(2,1)} copy(bf16[128,512]{1,0:T(8,128)(2,1)} %get-tuple-element.29) | data formatting | bytes 262144 | tf_op jit(solution)/shard_map/slice | solution.py:96
  71.5 1.7 %copy.76 = bf16[128,512]{0,1:T(8,128)(2,1)} copy(bf16[128,512]{1,0:T(8,128)(2,1)} %get-tuple-element.27) | data formatting | bytes 262144 | tf_op jit(solution)/shard_map/slice | solution.py:96
  73.2 1.4 %fusion.112 = (f32[8,128]{1,0:T(8,128)S(1)}, f32[8,128,128]{1,2,0:T(8,128)S(1)}) fusion(f32[8,128,128]{1,2,0:T(8,128)} %copy.87, bf16[128,8,64]{0,2,1:T(8,128)(2,1)} %bitcast.229, bf16[8,128,64]{1,2,0:T(8,128)(2,1)S(1)} %bitcast.223, pred[128,128]{0,1:T(8,128)(4,1)} %get-tuple-element.71), kind=kOutput, calls=%fused_computation.228 | convolution fusion | flops 17300480 | bytes 1331200 | tf_op jit(solution)/shard_map/hrd,chd->hrc/dot_general | solution.py:97
  74.6 1.4 %fusion.113 = (f32[8,128]{1,0:T(8,128)S(1)}, f32[8,128,128]{1,2,0:T(8,128)S(1)}) fusion(f32[8,128,128]{1,2,0:T(8,128)} %copy.86, bf16[128,8,64]{0,2,1:T(8,128)(2,1)} %bitcast.230, bf16[8,128,64]{1,2,0:T(8,128)(2,1)S(1)} %bitcast.224, pred[128,128]{0,1:T(8,128)(4,1)S(1)} %get-tuple-element.70), kind=kOutput, calls=%fused_computation.229 | convolution fusion | flops 17300480 | bytes 1331200 | tf_op jit(solution)/shard_map/hrd,chd->hrc/dot_general | solution.py:97
  76.1 0.7 fusion.102
  76.8 0.1 fusion.33
  76.9 0.1 fusion.35
  77.0 0.1 fusion.37
  77.4 0.2 fusion.26
  77.6 0.2 fusion.24
  77.9 0.2 fusion.22
  78.1 0.2 fusion.20
  78.3 0.2 fusion.27
  78.6 0.4 fusion.117
  79.0 0.2 multiply_reduce_fusion.1
  79.2 0.9 copy-done.2
  80.3 0.8 fusion.48
  81.1 0.1 fusion.32
  81.3 4.5 %collective-permute-start.4 = (bf16[60,1024]{1,0:T(8,128)(2,1)S(1)}, bf16[60,1024]{1,0:T(8,128)(2,1)S(1)}, u32[]{:S(2)}, u32[]{:S(2)}) collective-permute-start(bf16[60,1024]{1,0:T(8,128)(2,1)S(1)} %get-tuple-element.25), channel_id=1, source_target_pairs={{0,1},{1,2},{2,3},{3,4},{4,5},{5,6},{6,7},{7,8},{8,9},{9,10},{10,1... | collective-permute-start | bytes 368648 | tf_op jit(solution)/shard_map/ppermute | solution.py:29
  85.9 1.9 %collective-permute-start.5 = (bf16[60,1024]{1,0:T(8,128)(2,1)S(1)}, bf16[60,1024]{1,0:T(8,128)(2,1)S(1)}, u32[]{:S(2)}, u32[]{:S(2)}) collective-permute-start(bf16[60,1024]{1,0:T(8,128)(2,1)S(1)} %get-tuple-element.26), channel_id=1, source_target_pairs={{1,0},{2,1},{3,2},{4,3},{5,4},{6,5},{7,6},{8,7},{9,8},{10,9},{11,1... | collective-permute-start | bytes 368648 | tf_op jit(solution)/shard_map/ppermute | solution.py:31
  87.8 1.1 %fusion.111 = (f32[1,1024]{1,0:T(1,128)S(1)}, f32[1,1024]{1,0:T(1,128)S(1)}, f32[1,1024]{1,0:T(1,128)S(1)}, f32[1,1024]{1,0:T(1,128)S(1)}, f32[1,1024]{1,0:T(1,1...) fusion(f32[31,1024]{1,0:T(8,128)} %param.23), kind=kLoop, calls=%fused_computation.227 | loop fusion | bytes 98304 | tf_op jit(solution)/shard_map/slice | solution.py:150
  89.0 4.1 %collective-permute-done.5 = bf16[60,1024]{1,0:T(8,128)(2,1)S(1)} collective-permute-done((bf16[60,1024]{1,0:T(8,128)(2,1)S(1)}, bf16[60,1024]{1,0:T(8,128)(2,1)S(1)}, u32[]{:S(2)}, u32[]{:S(2)}) %collective-permute-start.5) | collective-permute-done | bytes 122912 | tf_op jit(solution)/shard_map/ppermute | solution.py:31
  93.2 2.5 %fusion.100 = (f32[128]{0:T(128)S(1)}, f32[128,1024]{1,0:T(8,128)S(1)}) fusion(bf16[60,1024]{1,0:T(8,128)(2,1)S(1)} %collective-permute-done.5, bf16[128,1024]{1,0:T(8,128)(2,1)S(1)} %fusion.32, f32[1024]{0:T(1024)S(1)} %bitcast.265, f32[1024]{0:T(1024)S(1)} %bitcast.266, f32[1024]{0:T(1024)S(1)} %bitcast.237, f32[1024]{0:T(1024)S(1)} %bitcast.238, ...), kind=kLoop, calls=%fused_computation.218 | loop fusion | flops 23986048 | bytes 1159680 | tf_op jit(solution)/shard_map/reduce_sum | solution.py:44
  95.8 0.2 multiply_reduce_fusion
  96.0 1.3 %fusion.16 = bf16[128,1024]{1,0:T(8,128)(2,1)} fusion(f32[128,1024]{1,0:T(8,128)S(1)} %get-tuple-element.85, bf16[1024,1024]{1,0:T(8,128)(2,1)S(1)} %copy-done, f32[128,1024]{1,0:T(8,128)S(1)} %get-tuple-element.11, f32[1024]{0:T(1024)S(1)} %copy-done.36, f32[128]{0:T(128)S(1)} %add_rsqrt_fusion, f32[128]{0:T(128)S(1)} %broadcast_multiply_fusion), kind=kOutput, calls=%fused_computation.51 | convolution fusion | flops 269746176 | bytes 3412992 | tf_op jit(solution)/shard_map/dot_general | solution.py:158
  (94 shorter events, 0.5 us)
Async XLA Ops:
  0.0 96.0 %copy-start = (bf16[1024,1024]{1,0:T(8,128)(2,1)S(1)}, bf16[1024,1024]{1,0:T(8,128)(2,1)}, u32[]{:S(2)}) copy-start(bf16[1024,1024]{1,0:T(8,128)(2,1)} %param.25) | copy-start | bytes 6291460
  3.3 41.8 %collective-permute-start.1 = (bf16[128,1024]{1,0:T(8,128)(2,1)}, bf16[128,1024]{1,0:T(8,128)(2,1)}, u32[]{:S(2)}, u32[]{:S(2)}) collective-permute-start(bf16[128,1024]{1,0:T(8,128)(2,1)} %constant_dynamic-update-slice_fusion), channel_id=1, source_target_pairs={{0,1},{1,2},{2,3},{3,4},{4,5},{5,6},{6,7},{7,8},{8,9},{9,10},{10,1... | collective-permute-start | bytes 786440 | tf_op jit(solution)/shard_map/ppermute | solution.py:18
  7.0 46.4 %collective-permute-start = (bf16[128,1024]{1,0:T(8,128)(2,1)}, bf16[128,1024]{1,0:T(8,128)(2,1)}, u32[]{:S(2)}, u32[]{:S(2)}) collective-permute-start(bf16[128,1024]{1,0:T(8,128)(2,1)} %constant_dynamic-update-slice_fusion), channel_id=1, source_target_pairs={{1,0},{2,1},{3,2},{4,3},{5,4},{6,5},{7,6},{8,7},{9,8},{10,9},{11,1... | collective-permute-start | bytes 786440 | tf_op jit(solution)/shard_map/ppermute | solution.py:18
  29.7 3.0 %copy-start.11 = (f32[31,1024]{1,0:T(8,128)S(1)}, f32[31,1024]{1,0:T(8,128)}, u32[]{:S(2)}) copy-start(f32[31,1024]{1,0:T(8,128)} %param.23) | copy-start | bytes 380932
  29.7 3.7 %copy-start.35 = (s32[128]{0:T(128)S(1)}, s32[128]{0:T(128)}, u32[]{:S(2)}) copy-start(s32[128]{0:T(128)} %compare_select_fusion.4) | copy-start | bytes 1540
  29.7 4.5 %copy-start.6 = (bf16[128,512]{1,0:T(8,128)(2,1)S(1)}, bf16[128,512]{1,0:T(8,128)(2,1)}, u32[]{:S(2)}) copy-start(bf16[128,512]{1,0:T(8,128)(2,1)} %param.15) | copy-start | bytes 393220
  29.7 5.3 %copy-start.7 = (bf16[128,512]{1,0:T(8,128)(2,1)S(1)}, bf16[128,512]{1,0:T(8,128)(2,1)}, u32[]{:S(2)}) copy-start(bf16[128,512]{1,0:T(8,128)(2,1)} %param.16) | copy-start | bytes 393220
  35.1 8.4 %copy-start.8 = (bf16[128,512]{0,1:T(8,128)(2,1)S(1)}, bf16[128,512]{0,1:T(8,128)(2,1)}, u32[]{:S(2)}) copy-start(bf16[128,512]{0,1:T(8,128)(2,1)} %copy.57) | copy-start | bytes 393220
  46.9 16.3 %collective-permute-start.3 = (bf16[128,1024]{1,0:T(8,128)(2,1)}, bf16[128,1024]{1,0:T(8,128)(2,1)}, u32[]{:S(2)}, u32[]{:S(2)}) collective-permute-start(bf16[128,1024]{1,0:T(8,128)(2,1)} %collective-permute-done.1), channel_id=1, source_target_pairs={{0,1},{1,2},{2,3},{3,4},{4,5},{5,6},{6,7},{7,8},{8,9},{9,10},{10,1... | collective-permute-start | bytes 786440 | tf_op jit(solution)/shard_map/ppermute | solution.py:18
  56.7 9.8 %collective-permute-start.2 = (bf16[128,1024]{1,0:T(8,128)(2,1)}, bf16[128,1024]{1,0:T(8,128)(2,1)}, u32[]{:S(2)}, u32[]{:S(2)}) collective-permute-start(bf16[128,1024]{1,0:T(8,128)(2,1)} %collective-permute-done), channel_id=1, source_target_pairs={{1,0},{2,1},{3,2},{4,3},{5,4},{6,5},{7,6},{8,7},{9,8},{10,9},{11,1... | collective-permute-start | bytes 786440 | tf_op jit(solution)/shard_map/ppermute | solution.py:18
  73.2 3.7 %copy-start.1 = (f32[8,128,128]{1,2,0:T(8,128)S(1)}, f32[8,128,128]{1,2,0:T(8,128)}, u32[]{:S(2)}) copy-start(f32[8,128,128]{1,2,0:T(8,128)} %get-tuple-element.81) | copy-start | bytes 1572868
  73.2 4.1 %copy-start.12 = (f32[8,128]{1,0:T(8,128)S(1)}, f32[8,128]{1,0:T(8,128)}, u32[]{:S(2)}) copy-start(f32[8,128]{1,0:T(8,128)} %get-tuple-element.82) | copy-start | bytes 12292
  73.2 4.1 %copy-start.13 = (f32[8,128]{1,0:T(8,128)S(1)}, f32[8,128]{1,0:T(8,128)}, u32[]{:S(2)}) copy-start(f32[8,128]{1,0:T(8,128)} %get-tuple-element.78) | copy-start | bytes 12292
  73.2 4.1 %copy-start.14 = (f32[8,128]{1,0:T(8,128)S(1)}, f32[8,128]{1,0:T(8,128)}, u32[]{:S(2)}) copy-start(f32[8,128]{1,0:T(8,128)} %get-tuple-element.80) | copy-start | bytes 12292
  73.2 4.4 %copy-start.4 = (bf16[128,512]{0,1:T(8,128)(2,1)S(1)}, bf16[128,512]{0,1:T(8,128)(2,1)}, u32[]{:S(2)}) copy-start(bf16[128,512]{0,1:T(8,128)(2,1)} %copy.64) | copy-start | bytes 393220
  76.1 2.0 %copy-start.5 = (bf16[128,512]{0,1:T(8,128)(2,1)S(1)}, bf16[128,512]{0,1:T(8,128)(2,1)}, u32[]{:S(2)}) copy-start(bf16[128,512]{0,1:T(8,128)(2,1)} %copy.72) | copy-start | bytes 393220
  77.0 1.3 %copy-start.10 = (bf16[128,512]{0,1:T(8,128)(2,1)S(1)}, bf16[128,512]{0,1:T(8,128)(2,1)}, u32[]{:S(2)}) copy-start(bf16[128,512]{0,1:T(8,128)(2,1)} %copy.76) | copy-start | bytes 393220
  77.2 1.4 %copy-start.3 = (bf16[512,1024]{1,0:T(8,128)(2,1)S(1)}, bf16[512,1024]{1,0:T(8,128)(2,1)}, u32[]{:S(2)}) copy-start(bf16[512,1024]{1,0:T(8,128)(2,1)} %param.20) | copy-start | bytes 3145732
  77.2 1.4 %copy-start.9 = (bf16[128,1024]{1,0:T(8,128)(2,1)S(1)}, bf16[128,1024]{1,0:T(8,128)(2,1)}, u32[]{:S(2)}) copy-start(bf16[128,1024]{1,0:T(8,128)(2,1)} %param.13) | copy-start | bytes 786436
  77.8 2.3 %copy-start.2 = (bf16[1024,2048]{1,0:T(8,128)(2,1)S(1)}, bf16[1024,2048]{1,0:T(8,128)(2,1)}, u32[]{:S(2)}) copy-start(bf16[1024,2048]{1,0:T(8,128)(2,1)} %param.22) | copy-start | bytes 12582916
  77.9 2.3 %copy-start.34 = (f32[1024]{0:T(1024)S(1)}, f32[1024]{0:T(1024)}, u32[]{:S(2)}) copy-start(f32[1024]{0:T(1024)} %param.21) | copy-start | bytes 12292
  80.1 12.9 %copy-start.15 = (f32[1,1024]{1,0:T(1,128)S(1)}, f32[1,1024]{1,0:T(1,128)}, u32[]{:S(2)}) copy-start(f32[1,1024]{1,0:T(1,128)} %get-tuple-element.35) | copy-start | bytes 12292
  80.2 12.9 %copy-start.16 = (f32[1,1024]{1,0:T(1,128)S(1)}, f32[1,1024]{1,0:T(1,128)}, u32[]{:S(2)}) copy-start(f32[1,1024]{1,0:T(1,128)} %get-tuple-element.36) | copy-start | bytes 12292
  80.2 12.9 %copy-start.17 = (f32[1,1024]{1,0:T(1,128)S(1)}, f32[1,1024]{1,0:T(1,128)}, u32[]{:S(2)}) copy-start(f32[1,1024]{1,0:T(1,128)} %get-tuple-element.37) | copy-start | bytes 12292
  80.2 12.9 %copy-start.18 = (f32[1,1024]{1,0:T(1,128)S(1)}, f32[1,1024]{1,0:T(1,128)}, u32[]{:S(2)}) copy-start(f32[1,1024]{1,0:T(1,128)} %get-tuple-element.38) | copy-start | bytes 12292
  80.2 12.9 %copy-start.19 = (f32[1,1024]{1,0:T(1,128)S(1)}, f32[1,1024]{1,0:T(1,128)}, u32[]{:S(2)}) copy-start(f32[1,1024]{1,0:T(1,128)} %get-tuple-element.39) | copy-start | bytes 12292
  80.2 12.9 %copy-start.20 = (f32[1,1024]{1,0:T(1,128)S(1)}, f32[1,1024]{1,0:T(1,128)}, u32[]{:S(2)}) copy-start(f32[1,1024]{1,0:T(1,128)} %get-tuple-element.40) | copy-start | bytes 12292
  80.2 12.9 %copy-start.21 = (f32[1,1024]{1,0:T(1,128)S(1)}, f32[1,1024]{1,0:T(1,128)}, u32[]{:S(2)}) copy-start(f32[1,1024]{1,0:T(1,128)} %get-tuple-element.41) | copy-start | bytes 12292
  80.2 12.9 %copy-start.22 = (f32[1,1024]{1,0:T(1,128)S(1)}, f32[1,1024]{1,0:T(1,128)}, u32[]{:S(2)}) copy-start(f32[1,1024]{1,0:T(1,128)} %get-tuple-element.42) | copy-start | bytes 12292
  80.2 12.9 %copy-start.23 = (f32[1,1024]{1,0:T(1,128)S(1)}, f32[1,1024]{1,0:T(1,128)}, u32[]{:S(2)}) copy-start(f32[1,1024]{1,0:T(1,128)} %get-tuple-element.43) | copy-start | bytes 12292
  80.2 12.9 %copy-start.24 = (f32[1,1024]{1,0:T(1,128)S(1)}, f32[1,1024]{1,0:T(1,128)}, u32[]{:S(2)}) copy-start(f32[1,1024]{1,0:T(1,128)} %get-tuple-element.44) | copy-start | bytes 12292
  80.2 12.9 %copy-start.25 = (f32[1,1024]{1,0:T(1,128)S(1)}, f32[1,1024]{1,0:T(1,128)}, u32[]{:S(2)}) copy-start(f32[1,1024]{1,0:T(1,128)} %get-tuple-element.45) | copy-start | bytes 12292
  80.2 12.9 %copy-start.26 = (f32[1,1024]{1,0:T(1,128)S(1)}, f32[1,1024]{1,0:T(1,128)}, u32[]{:S(2)}) copy-start(f32[1,1024]{1,0:T(1,128)} %get-tuple-element.46) | copy-start | bytes 12292
  80.2 12.9 %copy-start.27 = (f32[1,1024]{1,0:T(1,128)S(1)}, f32[1,1024]{1,0:T(1,128)}, u32[]{:S(2)}) copy-start(f32[1,1024]{1,0:T(1,128)} %get-tuple-element.47) | copy-start | bytes 12292
  80.3 12.9 %copy-start.28 = (f32[1,1024]{1,0:T(1,128)S(1)}, f32[1,1024]{1,0:T(1,128)}, u32[]{:S(2)}) copy-start(f32[1,1024]{1,0:T(1,128)} %get-tuple-element.48) | copy-start | bytes 12292
  80.3 12.9 %copy-start.29 = (f32[1,1024]{1,0:T(1,128)S(1)}, f32[1,1024]{1,0:T(1,128)}, u32[]{:S(2)}) copy-start(f32[1,1024]{1,0:T(1,128)} %get-tuple-element.49) | copy-start | bytes 12292
  80.3 12.9 %copy-start.30 = (f32[1,1024]{1,0:T(1,128)S(1)}, f32[1,1024]{1,0:T(1,128)}, u32[]{:S(2)}) copy-start(f32[1,1024]{1,0:T(1,128)} %get-tuple-element.50) | copy-start | bytes 12292
  80.3 12.9 %copy-start.31 = (f32[1,1024]{1,0:T(1,128)S(1)}, f32[1,1024]{1,0:T(1,128)}, u32[]{:S(2)}) copy-start(f32[1,1024]{1,0:T(1,128)} %get-tuple-element.51) | copy-start | bytes 12292
  80.3 12.9 %copy-start.32 = (f32[1,1024]{1,0:T(1,128)S(1)}, f32[1,1024]{1,0:T(1,128)}, u32[]{:S(2)}) copy-start(f32[1,1024]{1,0:T(1,128)} %get-tuple-element.52) | copy-start | bytes 12292
  80.3 12.9 %copy-start.33 = (f32[1,1024]{1,0:T(1,128)S(1)}, f32[1,1024]{1,0:T(1,128)}, u32[]{:S(2)}) copy-start(f32[1,1024]{1,0:T(1,128)} %get-tuple-element.53) | copy-start | bytes 12292
  81.1 14.9 %copy-start.36 = (f32[1024]{0:T(1024)S(1)}, f32[1024]{0:T(1024)}, u32[]{:S(2)}) copy-start(f32[1024]{0:T(1024)} %param.24) | copy-start | bytes 12292
  81.3 7.6 %collective-permute-start.4 = (bf16[60,1024]{1,0:T(8,128)(2,1)S(1)}, bf16[60,1024]{1,0:T(8,128)(2,1)S(1)}, u32[]{:S(2)}, u32[]{:S(2)}) collective-permute-start(bf16[60,1024]{1,0:T(8,128)(2,1)S(1)} %get-tuple-element.25), channel_id=1, source_target_pairs={{0,1},{1,2},{2,3},{3,4},{4,5},{5,6},{6,7},{7,8},{8,9},{9,10},{10,1... | collective-permute-start | bytes 368648 | tf_op jit(solution)/shard_map/ppermute | solution.py:29
  85.9 7.2 %collective-permute-start.5 = (bf16[60,1024]{1,0:T(8,128)(2,1)S(1)}, bf16[60,1024]{1,0:T(8,128)(2,1)S(1)}, u32[]{:S(2)}, u32[]{:S(2)}) collective-permute-start(bf16[60,1024]{1,0:T(8,128)(2,1)S(1)} %get-tuple-element.26), channel_id=1, source_target_pairs={{1,0},{2,1},{3,2},{4,3},{5,4},{6,5},{7,6},{8,7},{9,8},{10,9},{11,1... | collective-permute-start | bytes 368648 | tf_op jit(solution)/shard_map/ppermute | solution.py:31
where the time goes:
time: 98.3 us; the launch traced here: 97.3 us
  local copies, waits for them, and re-layouts  54.2 us (55%)
  starting transfers between devices  18.5 us (19%)
  matrix products  13.8 us (14%)
  other arithmetic  5.88 us (6%)
  waiting for transfers between devices  4.11 us (4%)
    unnamed x83, local copies, waits for them, and re-layouts  12.1 us
    ppermute x4, starting transfers between devices, shifted(): lax.ppermute(value, axis, [(source, source + steps) for source in range(l...  12.1 us
    slice x8, local copies, waits for them, and re-layouts, absorb(): packed_block[:, att_width:].reshape(row_count, head_count, head_width)  11.7 us
    dot_general x5, matrix products, absorb(): jnp.einsum('hrd,chd->hrc', queries, keys_here, preferred_element_type=jnp...  9.14 us
    reshape x1, local copies, waits for them, and re-layouts, on_device(): skewed.reshape(head_count, row_count, line_length - 1)[:, :, :window_cols]  6.98 us
    another operation x2, local copies, waits for them, and re-layouts, on_device(): repeated = jnp.tile(bias_line, (1, row_count + 1))  6.62 us
    slice x4, local copies, waits for them, and re-layouts, absorb(): packed_block[:, :att_width].reshape(row_count, head_count, head_width)  5.12 us
    ppermute x1, starting transfers between devices, padded_2(): lax.ppermute(tail, axis, [(i, (i + 1) % count) for i in range(ends)])  4.54 us
  transfers between devices with their start and end apart: 6, of which 1 were waited for; matrix products, arithmetic and copies ran while one was open for 54% of the time, Pallas kernels for 0%

commit v1 on v0

v1 whole, which is shorter than its diff:
```python
import functools

import jax
import jax.numpy as jnp
from jax import lax
from jax.experimental import pallas as pl
from jax.experimental.pallas import tpu as pltpu
from jax.sharding import PartitionSpec as P

KERNEL = 31
DILATION = 4
REACH = 2
SLOTS = 2 * REACH + 1
CHUNK = 128
GATE_COLS = 256
HALO = 64
CONV_ROWS = 32
CONV_COLS = 512

norm_epsilon = 1e-05
masked_score = -1e30


def layer_norm(values, gain_vec):
    row_mean = jnp.mean(values, axis=-1, keepdims=True)
    centred = values - row_mean
    spread = jnp.mean(centred * centred, axis=-1, keepdims=True)
    return centred * lax.rsqrt(spread + norm_epsilon) * gain_vec


def kernel(
    seq_count,
    lengths,
    table,
    bucket_bias,
    norm_gain,
    inner_gain,
    frames_hbm,
    query_hbm,
    key_hbm,
    value_hbm,
    out_w_hbm,
    expand_hbm,
    taps_hbm,
    shrink_hbm,
    out,
    frames,
    query,
    out_w,
    expand,
    taps,
    shrink,
    kv,
    table_pad,
    bias,
    attended,
    gated,
    plain,
    offset4,
    conv,
    local_sem,
    own_sem,
    p_send,
    p_recv,
    y_send,
    y_recv,
    z_send,
    z_recv,
    c_send,
    c_recv,
    h_send,
    h_recv,
):
    rows, width = frames.shape
    att_width = query.shape[1]
    chunks = att_width // CHUNK
    head_width = att_width // bucket_bias.shape[1]
    window = SLOTS * rows
    gate_chunks = width // GATE_COLS

    me = lax.axis_index("seq")
    core = lax.rem(me, 2)
    is_a = lax.rem(me, 4) < 2
    outer = is_a == (core == 0)
    partner = me + 1 - 2 * core
    y_peer = jnp.where(is_a, me + 2, me - 2)
    z_to = jnp.where(is_a, me + 4, me - 4)
    z_from = jnp.where(is_a, me - 4, me + 4)
    beside = jnp.where(core == 0, me - 1, me + 1)
    z_sends = jnp.logical_and(z_to >= 0, z_to < seq_count)
    z_gets = jnp.logical_and(z_from >= 0, z_from < seq_count)
    beside_is = jnp.logical_and(beside >= 0, beside < seq_count)
    c_sends = jnp.logical_or(outer, z_gets)
    c_gets = jnp.logical_or(jnp.logical_not(outer), z_gets)
    y_slot = jnp.where(is_a, 4, 0)
    z_slot = jnp.where(is_a, 0, 4)
    c_slot = jnp.where(core == 0, 1, 3)

    def slot_rows(slot):
        return pl.ds(pl.multiple_of(slot * rows, rows), rows)

    own = []
    for part, source in enumerate((key_hbm, value_hbm)):
        for g in range(chunks):
            own.append(
                pltpu.make_async_copy(
                    source.at[:, pl.ds(g * CHUNK, CHUNK)],
                    kv.at[g, part, pl.ds(REACH * rows, rows), :],
                    own_sem.at[g, part],
                )
            )
    local = [
        pltpu.make_async_copy(source, target, local_sem.at[i])
        for i, (source, target) in enumerate(
            (
                (query_hbm, query),
                (frames_hbm, frames),
                (out_w_hbm, out_w),
                (expand_hbm, expand),
                (taps_hbm, taps),
                (shrink_hbm, shrink),
            )
        )
    ]

    barrier = pltpu.get_barrier_semaphore()

    def greet(device):
        pl.semaphore_signal(
            barrier, inc=1, device_id={"seq": device}, device_id_type=pl.DeviceIdType.MESH
        )

    greet(partner)
    greet(y_peer)
    pl.when(z_sends)(lambda: greet(z_to))
    pl.when(z_gets)(lambda: greet(z_from))
    pl.when(beside_is)(lambda: greet(beside))
    for copy in own:
        copy.start()
    local[0].start()
    greetings = (
        2 + z_sends.astype(jnp.int32) + z_gets.astype(jnp.int32) + beside_is.astype(jnp.int32)
    )
    pl.semaphore_wait(barrier, greetings)

    def remote(source, target, send, recv, device):
        return pltpu.make_async_remote_copy(
            src_ref=source,
            dst_ref=target,
            send_sem=send,
            recv_sem=recv,
            device_id={"seq": device},
            device_id_type=pl.DeviceIdType.MESH,
        )

    def own_copy(g, part, slot, send, recv, device):
        source = (key_hbm, value_hbm)[part]
        return remote(
            source.at[:, pl.ds(g * CHUNK, CHUNK)],
            kv.at[g, part, slot_rows(slot), :],
            send.at[g, part],
            recv.at[g, part],
            device,
        )

    def relay(g, from_slot, to_slot, send, recv, device):
        return remote(
            kv.at[g, :, slot_rows(from_slot), :],
            kv.at[g, :, slot_rows(to_slot), :],
            send.at[g],
            recv.at[g],
            device,
        )

    def y_copy(g, part, slot):
        return own_copy(g, part, slot, y_send, y_recv, y_peer)

    def p_copy(g, part, slot):
        return own_copy(g, part, slot, p_send, p_recv, partner)

    y_target = jnp.where(is_a, 0, 4)
    p_target = 2 * core + 1
    p_slot = 3 - 2 * core
    c_target = jnp.where(core == 0, 3, 1)
    c_source = jnp.where(outer, y_slot, z_slot)

    def z_copy(g):
        return relay(g, y_slot, z_slot, z_send, z_recv, z_to)

    def c_copy(g, target):
        return relay(g, c_source, target, c_send, c_recv, partner)

    for g in range(chunks):
        for part in range(2):
            y_copy(g, part, y_target).start()
        for part in range(2):
            p_copy(g, part, p_target).start()
    for copy in local[1:]:
        copy.start()

    @pl.when(jnp.logical_not(z_gets))
    def _():
        for g in range(chunks):
            kv[g, :, slot_rows(z_slot), :] = jnp.zeros((2, rows, CHUNK), kv.dtype)

    @pl.when(jnp.logical_not(c_gets))
    def _():
        for g in range(chunks):
            kv[g, :, slot_rows(c_slot), :] = jnp.zeros((2, rows, CHUNK), kv.dtype)

    zero_halo = jnp.zeros((HALO, width), gated.dtype)

    @pl.when(me == 0)
    def _():
        gated[0:HALO, :] = zero_halo

    @pl.when(me == seq_count - 1)
    def _():
        gated[HALO + rows : 2 * HALO + rows, :] = zero_halo

    query_at = me * rows + lax.broadcasted_iota(jnp.int32, (rows, 1), 0)
    key_at = (me - REACH) * rows + lax.broadcasted_iota(jnp.int32, (1, window), 1)

    def count(u, state):
        bound, query_seg, key_seg = state
        bound = bound + lengths[u]
        return (
            bound,
            query_seg + (query_at >= bound).astype(jnp.int32),
            key_seg + (key_at >= bound).astype(jnp.int32),
        )

    utterances = lengths.shape[0]
    _, query_seg, key_seg = lax.fori_loop(
        0,
        utterances,
        count,
        (jnp.int32(0), jnp.zeros((rows, 1), jnp.int32), jnp.zeros((1, window), jnp.int32)),
        unroll=utterances <= 32,
    )
    key_seg = jnp.where(key_at < 0, -1, key_seg)

    line_length = table.shape[1]
    padded_length = window + rows
    table_pad[...] = jnp.zeros_like(table_pad)
    table_pad[:, 0:line_length] = table[...]
    buckets = bucket_bias.shape[0]
    hits = (
        lax.broadcasted_iota(jnp.int32, (buckets, padded_length), 0) == table_pad[...]
    ).astype(jnp.float32)
    bias_line = lax.dot_general(
        bucket_bias[...],
        hits,
        (((0,), (0,)), ((), ())),
        precision=lax.Precision.HIGHEST,
        preferred_element_type=jnp.float32,
    )
    heads_here = CHUNK // head_width

    def make_bias(g):
        same = query_seg == key_seg
        for h in range(heads_here):
            head = g * heads_here + h
            line = jnp.broadcast_to(bias_line[head : head + 1, :], (rows, padded_length))
            skewed = pltpu.roll(line, padded_length - (rows - 1), 1, stride=1, stride_axis=0)
            bias[g, h * rows : (h + 1) * rows, :] = jnp.where(
                same, skewed[:, :window], masked_score
            )

    head_of_lane = lax.broadcasted_iota(jnp.int32, (rows, CHUNK), 1) // head_width

    def attend(g):
        for part in range(2):
            own[part * chunks + g].wait()
            p_copy(g, part, p_slot).wait_recv()

        @pl.when(c_gets)
        def _():
            c_copy(g, c_slot).wait_recv()

        chunk_query = query[:, g * CHUNK : (g + 1) * CHUNK]
        stacked = jnp.concatenate(
            [
                jnp.where(head_of_lane == h, chunk_query, jnp.zeros_like(chunk_query))
                for h in range(heads_here)
            ],
            axis=0,
        )
        scores = lax.dot_general(
            stacked, kv[g, 0], (((1,), (1,)), ((), ())), preferred_element_type=jnp.float32
        )
        scores = scores * (head_width**-0.5) + bias[g]
        top = jnp.max(scores, axis=1, keepdims=True)
        weights = jnp.exp(scores - top)
        row_total = jnp.sum(weights, axis=1, keepdims=True)
        weighted = jnp.dot(
            weights.astype(jnp.bfloat16), kv[g, 1], preferred_element_type=jnp.float32
        )
        normal = (weighted / row_total).astype(jnp.bfloat16)
        result = normal[0:rows]
        for h in range(1, heads_here):
            result = jnp.where(head_of_lane == h, normal[h * rows : (h + 1) * rows], result)
        attended[:, g * CHUNK : (g + 1) * CHUNK] = result

    def pass_z(g):
        @pl.when(z_gets)
        def _():
            relay(g, y_slot, z_slot, z_send, z_recv, z_to).wait_recv()

        @pl.when(jnp.logical_and(z_gets, jnp.logical_not(outer)))
        def _():
            c_copy(g, c_target).start()

    local[0].wait()
    for g in range(chunks):
        make_bias(g)
        for part in range(2):
            y_copy(g, part, y_slot).wait_recv()
        pl.when(z_sends)(lambda g=g: z_copy(g).start())
        pl.when(outer)(lambda g=g: c_copy(g, c_target).start())
        if g >= 1:
            pass_z(g - 1)
        if g >= 2:
            attend(g - 2)
    pass_z(chunks - 1)
    for g in range(max(0, chunks - 2), chunks):
        attend(g)

    local[1].wait()
    local[2].wait()
    mid = (
        frames[...].astype(jnp.float32)
        + jnp.dot(attended[...], out_w[...], preferred_element_type=jnp.float32)
    ).astype(jnp.bfloat16)
    frames[...] = mid
    normed = layer_norm(mid.astype(jnp.float32), norm_gain[...]).astype(jnp.bfloat16)
    local[3].wait()

    def to_prev(j):
        cols = pl.ds(j * GATE_COLS, GATE_COLS)
        return remote(
            gated.at[pl.ds(HALO, HALO), cols],
            gated.at[pl.ds(HALO + rows, HALO), cols],
            h_send.at[0, j],
            h_recv.at[0, j],
            me - 1,
        )

    def to_next(j):
        cols = pl.ds(j * GATE_COLS, GATE_COLS)
        return remote(
            gated.at[pl.ds(rows, HALO), cols],
            gated.at[pl.ds(0, HALO), cols],
            h_send.at[1, j],
            h_recv.at[1, j],
            me + 1,
        )

    has_prev = me > 0
    has_next = me < seq_count - 1
    for j in range(gate_chunks):
        first = j * GATE_COLS
        cols = slice(first, first + GATE_COLS)
        linear = jnp.dot(normed, expand[:, cols], preferred_element_type=jnp.float32)
        gate = jnp.dot(
            normed,
            expand[:, width + first : width + first + GATE_COLS],
            preferred_element_type=jnp.float32,
        )
        units = (linear * jax.nn.sigmoid(gate)).astype(jnp.bfloat16)
        gated[HALO : HALO + rows, cols] = units
        pl.when(has_prev)(lambda j=j: to_prev(j).start())
        pl.when(has_next)(lambda j=j: to_next(j).start())
        wide = units.astype(jnp.float32)
        plain[HALO : HALO + rows, cols] = wide
        offset4[HALO - 4 : HALO - 4 + rows, cols] = wide

    local[4].wait()

    def first_row(i, t):
        return i * CONV_ROWS + HALO + DILATION * (t - KERNEL // 2)

    def is_own(i, t):
        return first_row(i, t) >= HALO and first_row(i, t) + CONV_ROWS <= HALO + rows

    def add_taps(total, i, cols, chosen):
        for t in chosen:
            row = first_row(i, t)
            source = plain if row % 8 == 0 else offset4
            row -= row % 8
            term = taps[t : t + 1, cols] * source[row : row + CONV_ROWS, cols]
            total = term if total is None else total + term
        return total

    tiles = [
        (i, slice(c * CONV_COLS, (c + 1) * CONV_COLS))
        for c in range(width // CONV_COLS)
        for i in range(rows // CONV_ROWS)
    ]
    for i, cols in tiles:
        conv[i * CONV_ROWS : (i + 1) * CONV_ROWS, cols] = add_taps(
            None, i, cols, [t for t in range(KERNEL) if is_own(i, t)]
        )

    for j in range(gate_chunks):
        pl.when(has_next)(lambda j=j: to_prev(j).wait_recv())
        pl.when(has_prev)(lambda j=j: to_next(j).wait_recv())
    left = gated[0:HALO, :].astype(jnp.float32)
    right = gated[HALO + rows : 2 * HALO + rows, :].astype(jnp.float32)
    plain[0:HALO, :] = left
    plain[HALO + rows : 2 * HALO + rows, :] = right
    offset4[0 : HALO - 4, :] = left[4:HALO]
    offset4[HALO - 4 + rows : 2 * HALO - 4 + rows, :] = right
    for i, cols in tiles:
        here = slice(i * CONV_ROWS, (i + 1) * CONV_ROWS)
        conv[here, cols] = add_taps(
            conv[here, cols], i, cols, [t for t in range(KERNEL) if not is_own(i, t)]
        )

    inner = layer_norm(conv[...], inner_gain[...])
    activated = (inner * jax.nn.sigmoid(inner)).astype(jnp.bfloat16)
    local[5].wait()
    out[...] = (
        frames[...].astype(jnp.float32)
        + jnp.dot(activated, shrink[...], preferred_element_type=jnp.float32)
    ).astype(jnp.bfloat16)

    for g in range(chunks):
        for part in range(2):
            y_copy(g, part, y_target).wait_send()
            p_copy(g, part, p_target).wait_send()
        pl.when(z_sends)(lambda g=g: z_copy(g).wait_send())
        pl.when(c_sends)(lambda g=g: c_copy(g, c_target).wait_send())
    for j in range(gate_chunks):
        pl.when(has_prev)(lambda j=j: to_prev(j).wait_send())
        pl.when(has_next)(lambda j=j: to_next(j).wait_send())


def on_device(
    frames_in,
    query_proj,
    key_proj,
    value_proj,
    utterance_lengths,
    bucket_table,
    bucket_bias,
    out_weight,
    norm_gain,
    expand_weight,
    depth_taps,
    inner_gain,
    shrink_weight,
):
    rows, width = frames_in.shape
    att_width = query_proj.shape[1]
    chunks = att_width // CHUNK
    gate_chunks = width // GATE_COLS
    window = SLOTS * rows
    heads_here = CHUNK // (att_width // bucket_bias.shape[1])
    wide_rows = rows + 2 * HALO
    bf16, f32 = jnp.bfloat16, jnp.float32
    vmem = pl.BlockSpec(memory_space=pltpu.VMEM)
    anywhere = pl.BlockSpec(memory_space=pl.ANY)
    dma = pltpu.SemaphoreType.DMA
    return pl.pallas_call(
        functools.partial(kernel, lax.axis_size("seq")),
        out_shape=jax.ShapeDtypeStruct((rows, width), bf16),
        in_specs=[pl.BlockSpec(memory_space=pltpu.SMEM)] + [vmem] * 4 + [anywhere] * 8,
        out_specs=vmem,
        scratch_shapes=[
            pltpu.VMEM((rows, width), bf16),
            pltpu.VMEM((rows, att_width), bf16),
            pltpu.VMEM(out_weight.shape, bf16),
            pltpu.VMEM(expand_weight.shape, bf16),
            pltpu.VMEM(depth_taps.shape, f32),
            pltpu.VMEM(shrink_weight.shape, bf16),
            pltpu.VMEM((chunks, 2, window, CHUNK), bf16),
            pltpu.VMEM((1, window + rows), jnp.int32),
            pltpu.VMEM((chunks, heads_here * rows, window), f32),
            pltpu.VMEM((rows, att_width), bf16),
            pltpu.VMEM((wide_rows, width), bf16),
            pltpu.VMEM((wide_rows, width), f32),
            pltpu.VMEM((wide_rows, width), f32),
            pltpu.VMEM((rows, width), f32),
            dma((6,)),
            dma((chunks, 2)),
            dma((chunks, 2)),
            dma((chunks, 2)),
            dma((chunks, 2)),
            dma((chunks, 2)),
            dma((chunks,)),
            dma((chunks,)),
            dma((chunks,)),
            dma((chunks,)),
            dma((2, gate_chunks)),
            dma((2, gate_chunks)),
        ],
        compiler_params=pltpu.CompilerParams(
            collective_id=0, has_side_effects=True, vmem_limit_bytes=40 * 1024 * 1024
        ),
    )(
        utterance_lengths,
        bucket_table.reshape(1, -1),
        bucket_bias,
        norm_gain.reshape(1, -1),
        inner_gain.reshape(1, -1),
        frames_in,
        query_proj,
        key_proj,
        value_proj,
        out_weight,
        expand_weight,
        depth_taps,
        shrink_weight,
    )


def solution(mesh):
    placed = (
        P(("groups", "seq"), None),
        P(("groups", "seq"), None),
        P(("groups", "seq"), None),
        P(("groups", "seq"), None),
        P("groups"),
        P(),
        P(),
        P(),
        P(),
        P(),
        P(),
        P(),
        P(),
    )
    return jax.shard_map(
        on_device, mesh=mesh, in_specs=placed, out_specs=P(("groups", "seq"), None), check_vma=False
    )
```

time: 98.3 us -> 39.5 us (0.40)
  the two profiles are of different devices: /device:TPU:21 before, /device:TPU:11 now
where the time goes in v1:
time: 39.5 us; the launch traced here: 39.1 us
  Pallas kernels  25.3 us (64%)
  local copies, waits for them, and re-layouts  13.7 us (35%)
    pallas_call x1, Pallas kernels, on_device(): pl.pallas_call(functools.partial(kernel, lax.axis_size('seq')), out_shape...  25.3 us
    unnamed x24, local copies, waits for them, and re-layouts  13.1 us

profile of v1, /device:TPU:11, one launch (start us, length us, event | category | flops | bytes accessed | tf_op | source)
XLA Modules:
  0.0 39.1 jit_solution(5504764573582500784)
XLA Ops:
  0.0 0.7 %reshape.9.table = s32[1,767]{1,0:T(1,128)S(1)} reshape(s32[767]{0:T(1024)} %param.18) | data formatting | bytes 6136 | tf_op jit(solution)/shard_map/reshape | solution.py:503
  0.7 0.8 %copy.14.bucket_bias = f32[32,8]{1,0:T(8,128)S(1)} copy(f32[32,8]{0,1:T(8,128)} %param.19) | data formatting | bytes 2048 | tf_op args[6]
  1.5 0.0 copy-start
  1.5 2.2 %copy-done = bf16[1024,2048]{1,0:T(8,128)(2,1)S(1)} copy-done((bf16[1024,2048]{1,0:T(8,128)(2,1)S(1)}, bf16[1024,2048]{1,0:T(8,128)(2,1)}, u32[]{:S(2)}) %copy-start) | copy-done | bytes 4194328
  3.6 0.0 copy-start.1
  3.6 1.6 %copy-done.1 = bf16[1024,1024]{1,0:T(8,128)(2,1)S(1)} copy-done((bf16[1024,1024]{1,0:T(8,128)(2,1)S(1)}, bf16[1024,1024]{1,0:T(8,128)(2,1)}, u32[]{:S(2)}) %copy-start.1) | copy-done | bytes 2097176
  5.2 0.0 copy-start.2
  5.2 1.2 %copy-done.2 = bf16[512,1024]{1,0:T(8,128)(2,1)S(1)} copy-done((bf16[512,1024]{1,0:T(8,128)(2,1)S(1)}, bf16[512,1024]{1,0:T(8,128)(2,1)}, u32[]{:S(2)}) %copy-start.2) | copy-done | bytes 1048600
  6.5 0.0 copy-start.3
  6.5 0.9 %copy-done.3 = bf16[128,1024]{1,0:T(8,128)(2,1)S(1)} copy-done((bf16[128,1024]{1,0:T(8,128)(2,1)S(1)}, bf16[128,1024]{1,0:T(8,128)(2,1)}, u32[]{:S(2)}) %copy-start.3) | copy-done | bytes 262168
  7.4 0.0 copy-start.4
  7.4 0.9 %copy-done.4 = bf16[128,512]{1,0:T(8,128)(2,1)S(1)} copy-done((bf16[128,512]{1,0:T(8,128)(2,1)S(1)}, bf16[128,512]{1,0:T(8,128)(2,1)}, u32[]{:S(2)}) %copy-start.4) | copy-done | bytes 131096
  8.3 0.0 copy-start.5
  8.3 0.9 %copy-done.5 = bf16[128,512]{1,0:T(8,128)(2,1)S(1)} copy-done((bf16[128,512]{1,0:T(8,128)(2,1)S(1)}, bf16[128,512]{1,0:T(8,128)(2,1)}, u32[]{:S(2)}) %copy-start.5) | copy-done | bytes 131096
  9.2 0.0 copy-start.6
  9.2 0.9 %copy-done.6 = bf16[128,512]{1,0:T(8,128)(2,1)S(1)} copy-done((bf16[128,512]{1,0:T(8,128)(2,1)S(1)}, bf16[128,512]{1,0:T(8,128)(2,1)}, u32[]{:S(2)}) %copy-start.6) | copy-done | bytes 131096
  10.1 0.0 copy-start.7
  10.1 0.9 %copy-done.7 = f32[31,1024]{1,0:T(8,128)S(1)} copy-done((f32[31,1024]{1,0:T(8,128)S(1)}, f32[31,1024]{1,0:T(8,128)}, u32[]{:S(2)}) %copy-start.7) | copy-done | bytes 127000
  11.0 0.0 copy-start.8
  11.0 0.7 %copy-done.8 = f32[1024]{0:T(1024)S(1)} copy-done((f32[1024]{0:T(1024)S(1)}, f32[1024]{0:T(1024)}, u32[]{:S(2)}) %copy-start.8) | copy-done | bytes 4120
  11.7 0.0 copy-start.9
  11.7 0.7 %copy-done.9 = f32[1024]{0:T(1024)S(1)} copy-done((f32[1024]{0:T(1024)S(1)}, f32[1024]{0:T(1024)}, u32[]{:S(2)}) %copy-start.9) | copy-done | bytes 4120
  12.4 0.0 copy-start.10
  12.4 0.7 %copy-done.10 = s32[16]{0:T(128)S(1)} copy-done((s32[16]{0:T(128)S(1)}, s32[16]{0:T(128)}, u32[]{:S(2)}) %copy-start.10) | copy-done | bytes 88
  13.1 25.3 %shard_map.127 = bf16[128,1024]{1,0:T(8,128)(2,1)S(1)} custom-call(s32[16]{0:T(128)S(1)} %copy-done.10, s32[1,767]{1,0:T(1,128)S(1)} %reshape.9.table, f32[32,8]{1,0:T(8,128)S(1)} %copy.14.bucket_bias, f32[1,1024]{1,0:T(1,128)S(1)} %bitcast.2, f32[1,1024]{1,0:T(1,128)S(1)} %bitcast.3, bf16[128,1024]{1,0:T(8,128)(2,1)S(1)} %copy-done.3, ...), custom_call_target="tpu_custom_call" | custom-call | tf_op jit(solution)/shard_map/pallas_call | solution.py:465
  38.4 0.7 %copy.16 = bf16[128,1024]{1,0:T(8,128)(2,1)} copy(bf16[128,1024]{1,0:T(8,128)(2,1)S(1)} %shard_map.127) | data formatting | bytes 524288
Async XLA Ops:
  1.5 2.2 %copy-start = (bf16[1024,2048]{1,0:T(8,128)(2,1)S(1)}, bf16[1024,2048]{1,0:T(8,128)(2,1)}, u32[]{:S(2)}) copy-start(bf16[1024,2048]{1,0:T(8,128)(2,1)} %expand_hbm.1) | copy-start | bytes 12582916
  3.6 1.6 %copy-start.1 = (bf16[1024,1024]{1,0:T(8,128)(2,1)S(1)}, bf16[1024,1024]{1,0:T(8,128)(2,1)}, u32[]{:S(2)}) copy-start(bf16[1024,1024]{1,0:T(8,128)(2,1)} %shrink_hbm.1) | copy-start | bytes 6291460
  5.2 1.2 %copy-start.2 = (bf16[512,1024]{1,0:T(8,128)(2,1)S(1)}, bf16[512,1024]{1,0:T(8,128)(2,1)}, u32[]{:S(2)}) copy-start(bf16[512,1024]{1,0:T(8,128)(2,1)} %out_w_hbm.1) | copy-start | bytes 3145732
  6.5 0.9 %copy-start.3 = (bf16[128,1024]{1,0:T(8,128)(2,1)S(1)}, bf16[128,1024]{1,0:T(8,128)(2,1)}, u32[]{:S(2)}) copy-start(bf16[128,1024]{1,0:T(8,128)(2,1)} %frames_hbm.1) | copy-start | bytes 786436
  7.4 0.9 %copy-start.4 = (bf16[128,512]{1,0:T(8,128)(2,1)S(1)}, bf16[128,512]{1,0:T(8,128)(2,1)}, u32[]{:S(2)}) copy-start(bf16[128,512]{1,0:T(8,128)(2,1)} %query_hbm.1) | copy-start | bytes 393220
  8.3 0.9 %copy-start.5 = (bf16[128,512]{1,0:T(8,128)(2,1)S(1)}, bf16[128,512]{1,0:T(8,128)(2,1)}, u32[]{:S(2)}) copy-start(bf16[128,512]{1,0:T(8,128)(2,1)} %key_hbm.1) | copy-start | bytes 393220
  9.2 0.9 %copy-start.6 = (bf16[128,512]{1,0:T(8,128)(2,1)S(1)}, bf16[128,512]{1,0:T(8,128)(2,1)}, u32[]{:S(2)}) copy-start(bf16[128,512]{1,0:T(8,128)(2,1)} %value_hbm.1) | copy-start | bytes 393220
  10.1 0.9 %copy-start.7 = (f32[31,1024]{1,0:T(8,128)S(1)}, f32[31,1024]{1,0:T(8,128)}, u32[]{:S(2)}) copy-start(f32[31,1024]{1,0:T(8,128)} %taps_hbm.1) | copy-start | bytes 380932
  11.0 0.7 %copy-start.8 = (f32[1024]{0:T(1024)S(1)}, f32[1024]{0:T(1024)}, u32[]{:S(2)}) copy-start(f32[1024]{0:T(1024)} %param.21) | copy-start | bytes 12292
  11.7 0.7 %copy-start.9 = (f32[1024]{0:T(1024)S(1)}, f32[1024]{0:T(1024)}, u32[]{:S(2)}) copy-start(f32[1024]{0:T(1024)} %param.24) | copy-start | bytes 12292
  12.4 0.7 %copy-start.10 = (s32[16]{0:T(128)S(1)}, s32[16]{0:T(128)}, u32[]{:S(2)}) copy-start(s32[16]{0:T(128)} %lengths.1) | copy-start | bytes 196

commit v2 on v1

--- a/solution.py
+++ b/solution.py
@@ -30,11 +30,11 @@
 
 def kernel(
     seq_count,
-    lengths,
-    table,
-    bucket_bias,
-    norm_gain,
-    inner_gain,
+    lengths_hbm,
+    table_hbm,
+    bucket_bias_hbm,
+    norm_gain_hbm,
+    inner_gain_hbm,
     frames_hbm,
     query_hbm,
     key_hbm,
@@ -44,6 +44,11 @@
     taps_hbm,
     shrink_hbm,
     out,
+    lengths,
+    table,
+    bucket_bias,
+    norm_gain,
+    inner_gain,
     frames,
     query,
     out_w,
@@ -74,7 +79,7 @@
     rows, width = frames.shape
     att_width = query.shape[1]
     chunks = att_width // CHUNK
-    head_width = att_width // bucket_bias.shape[1]
+    head_width = att_width // bucket_bias.shape[0]
     window = SLOTS * rows
     gate_chunks = width // GATE_COLS
 
@@ -113,11 +118,16 @@
         pltpu.make_async_copy(source, target, local_sem.at[i])
         for i, (source, target) in enumerate(
             (
+                (lengths_hbm, lengths),
+                (table_hbm, table),
+                (bucket_bias_hbm, bucket_bias),
                 (query_hbm, query),
                 (frames_hbm, frames),
                 (out_w_hbm, out_w),
+                (norm_gain_hbm, norm_gain),
                 (expand_hbm, expand),
                 (taps_hbm, taps),
+                (inner_gain_hbm, inner_gain),
                 (shrink_hbm, shrink),
             )
         )
@@ -135,9 +145,8 @@
     pl.when(z_sends)(lambda: greet(z_to))
     pl.when(z_gets)(lambda: greet(z_from))
     pl.when(beside_is)(lambda: greet(beside))
-    for copy in own:
+    for copy in local[:4] + own:
         copy.start()
-    local[0].start()
     greetings = (
         2 + z_sends.astype(jnp.int32) + z_gets.astype(jnp.int32) + beside_is.astype(jnp.int32)
     )
@@ -195,7 +204,7 @@
             y_copy(g, part, y_target).start()
         for part in range(2):
             p_copy(g, part, p_target).start()
-    for copy in local[1:]:
+    for copy in local[4:]:
         copy.start()
 
     @pl.when(jnp.logical_not(z_gets))
@@ -217,6 +226,9 @@
     @pl.when(me == seq_count - 1)
     def _():
         gated[HALO + rows : 2 * HALO + rows, :] = zero_halo
+
+    for copy in local[:3]:
+        copy.wait()
 
     query_at = me * rows + lax.broadcasted_iota(jnp.int32, (rows, 1), 0)
     key_at = (me - REACH) * rows + lax.broadcasted_iota(jnp.int32, (1, window), 1)
@@ -240,18 +252,17 @@
     )
     key_seg = jnp.where(key_at < 0, -1, key_seg)
 
-    line_length = table.shape[1]
+    line_length = table.shape[0]
     padded_length = window + rows
     table_pad[...] = jnp.zeros_like(table_pad)
-    table_pad[:, 0:line_length] = table[...]
-    buckets = bucket_bias.shape[0]
+    table_pad[:, 0:line_length] = table[...].reshape(1, line_length)
+    buckets = bucket_bias.shape[1]
     hits = (
         lax.broadcasted_iota(jnp.int32, (buckets, padded_length), 0) == table_pad[...]
     ).astype(jnp.float32)
-    bias_line = lax.dot_general(
+    bias_line = jnp.dot(
         bucket_bias[...],
         hits,
-        (((0,), (0,)), ((), ())),
         precision=lax.Precision.HIGHEST,
         preferred_element_type=jnp.float32,
     )
@@ -292,11 +303,11 @@
         scores = scores * (head_width**-0.5) + bias[g]
         top = jnp.max(scores, axis=1, keepdims=True)
         weights = jnp.exp(scores - top)
-        row_total = jnp.sum(weights, axis=1, keepdims=True)
+        values_and_ones = jnp.concatenate([kv[g, 1], jnp.ones_like(kv[g, 1])], axis=1)
         weighted = jnp.dot(
-            weights.astype(jnp.bfloat16), kv[g, 1], preferred_element_type=jnp.float32
-        )
-        normal = (weighted / row_total).astype(jnp.bfloat16)
+            weights.astype(jnp.bfloat16), values_and_ones, preferred_element_type=jnp.float32
+        )
+        normal = (weighted[:, :CHUNK] / weighted[:, CHUNK:]).astype(jnp.bfloat16)
         result = normal[0:rows]
         for h in range(1, heads_here):
             result = jnp.where(head_of_lane == h, normal[h * rows : (h + 1) * rows], result)
@@ -311,7 +322,7 @@
         def _():
             c_copy(g, c_target).start()
 
-    local[0].wait()
+    local[3].wait()
     for g in range(chunks):
         make_bias(g)
         for part in range(2):
@@ -326,15 +337,15 @@
     for g in range(max(0, chunks - 2), chunks):
         attend(g)
 
-    local[1].wait()
-    local[2].wait()
+    for copy in local[4:7]:
+        copy.wait()
     mid = (
         frames[...].astype(jnp.float32)
         + jnp.dot(attended[...], out_w[...], preferred_element_type=jnp.float32)
     ).astype(jnp.bfloat16)
     frames[...] = mid
     normed = layer_norm(mid.astype(jnp.float32), norm_gain[...]).astype(jnp.bfloat16)
-    local[3].wait()
+    local[7].wait()
 
     def to_prev(j):
         cols = pl.ds(j * GATE_COLS, GATE_COLS)
@@ -375,7 +386,7 @@
         plain[HALO : HALO + rows, cols] = wide
         offset4[HALO - 4 : HALO - 4 + rows, cols] = wide
 
-    local[4].wait()
+    local[8].wait()
 
     def first_row(i, t):
         return i * CONV_ROWS + HALO + DILATION * (t - KERNEL // 2)
@@ -417,9 +428,10 @@
             conv[here, cols], i, cols, [t for t in range(KERNEL) if not is_own(i, t)]
         )
 
+    local[9].wait()
     inner = layer_norm(conv[...], inner_gain[...])
     activated = (inner * jax.nn.sigmoid(inner)).astype(jnp.bfloat16)
-    local[5].wait()
+    local[10].wait()
     out[...] = (
         frames[...].astype(jnp.float32)
         + jnp.dot(activated, shrink[...], preferred_element_type=jnp.float32)
@@ -465,9 +477,14 @@
     return pl.pallas_call(
         functools.partial(kernel, lax.axis_size("seq")),
         out_shape=jax.ShapeDtypeStruct((rows, width), bf16),
-        in_specs=[pl.BlockSpec(memory_space=pltpu.SMEM)] + [vmem] * 4 + [anywhere] * 8,
+        in_specs=[anywhere] * 13,
         out_specs=vmem,
         scratch_shapes=[
+            pltpu.SMEM(utterance_lengths.shape, jnp.int32),
+            pltpu.VMEM(bucket_table.shape, jnp.int32),
+            pltpu.VMEM(bucket_bias.shape[::-1], f32),
+            pltpu.VMEM((1, width), f32),
+            pltpu.VMEM((1, width), f32),
             pltpu.VMEM((rows, width), bf16),
             pltpu.VMEM((rows, att_width), bf16),
             pltpu.VMEM(out_weight.shape, bf16),
@@ -482,7 +499,7 @@
             pltpu.VMEM((wide_rows, width), f32),
             pltpu.VMEM((wide_rows, width), f32),
             pltpu.VMEM((rows, width), f32),
-            dma((6,)),
+            dma((11,)),
             dma((chunks, 2)),
             dma((chunks, 2)),
             dma((chunks, 2)),
@@ -496,12 +513,12 @@
             dma((2, gate_chunks)),
         ],
         compiler_params=pltpu.CompilerParams(
-            collective_id=0, has_side_effects=True, vmem_limit_bytes=40 * 1024 * 1024
+            collective_id=0, has_side_effects=True, vmem_limit_bytes=60 * 1024 * 1024
         ),
     )(
         utterance_lengths,
-        bucket_table.reshape(1, -1),
-        bucket_bias,
+        bucket_table,
+        bucket_bias.T,
         norm_gain.reshape(1, -1),
         inner_gain.reshape(1, -1),
         frames_in,

time: 39.5 us -> 27.7 us (0.70)
  local copies, waits for them, and re-layouts: 13.7 us -> 1.67 us
  Pallas kernels: 25.3 us -> 25.9 us
    unnamed x24 -> x1, local copies, waits for them, and re-layouts: 13.1 us -> 1.67 us
    reshape x1 -> x0, local copies, waits for them, and re-layouts: 0.69 us -> none  [on_device(): bucket_table.reshape(1, -1)]
    pallas_call x1, Pallas kernels: 25.3 us -> 25.9 us  [on_device(): pl.pallas_call(functools.partial(kernel, lax.axis_size('seq')), out_shape...]
where the time goes in v2:
time: 27.7 us; the launch traced here: 27.6 us
  Pallas kernels  25.9 us (94%)
  local copies, waits for them, and re-layouts  1.67 us (6%)
    pallas_call x1, Pallas kernels, on_device(): pl.pallas_call(functools.partial(kernel, lax.axis_size('seq')), out_shape...  25.9 us
    unnamed x1, local copies, waits for them, and re-layouts  1.67 us

profile of v2, /device:TPU:11, one launch (start us, length us, event | category | flops | bytes accessed | tf_op | source)
XLA Modules:
  0.0 27.6 jit_solution(7219591271069080765)
XLA Ops:
  0.0 25.9 %shard_map.127 = bf16[128,1024]{1,0:T(8,128)(2,1)} custom-call(s32[16]{0:T(128)} %lengths_hbm.1, s32[767]{0:T(1024)} %table_hbm.1, f32[8,32]{1,0:T(8,128)} %bitcast.3, f32[1,1024]{1,0:T(1,128)} %bitcast.4, f32[1,1024]{1,0:T(1,128)} %bitcast.5, bf16[128,1024]{1,0:T(8,128)(2,1)} %frames_hbm.1, bf16[128,512]{1,0:T(8,128)(2,1)} %query_hbm.1, ...), custom_call_target="tpu_custom_call" | custom-call | tf_op jit(solution)/shard_map/pallas_call | solution.py:477
  25.9 1.7 %copy.15 = bf16[128,1024]{1,0:T(8,128)(2,1)} copy(bf16[128,1024]{1,0:T(8,128)(2,1)} %shard_map.127) | data formatting | bytes 524288

commit v3 on v2

--- a/solution.py
+++ b/solution.py
@@ -63,6 +63,7 @@
     plain,
     offset4,
     conv,
+    result,
     local_sem,
     own_sem,
     p_send,
@@ -75,6 +76,7 @@
     c_recv,
     h_send,
     h_recv,
+    out_sem,
 ):
     rows, width = frames.shape
     att_width = query.shape[1]
@@ -172,12 +174,12 @@
             device,
         )
 
-    def relay(g, from_slot, to_slot, send, recv, device):
+    def relay(g, part, from_slot, to_slot, send, recv, device):
         return remote(
-            kv.at[g, :, slot_rows(from_slot), :],
-            kv.at[g, :, slot_rows(to_slot), :],
-            send.at[g],
-            recv.at[g],
+            kv.at[g, part, slot_rows(from_slot), :],
+            kv.at[g, part, slot_rows(to_slot), :],
+            send.at[g, part],
+            recv.at[g, part],
             device,
         )
 
@@ -193,11 +195,11 @@
     c_target = jnp.where(core == 0, 3, 1)
     c_source = jnp.where(outer, y_slot, z_slot)
 
-    def z_copy(g):
-        return relay(g, y_slot, z_slot, z_send, z_recv, z_to)
-
-    def c_copy(g, target):
-        return relay(g, c_source, target, c_send, c_recv, partner)
+    def z_copy(g, part):
+        return relay(g, part, y_slot, z_slot, z_send, z_recv, z_to)
+
+    def c_copy(g, part, target):
+        return relay(g, part, c_source, target, c_send, c_recv, partner)
 
     for g in range(chunks):
         for part in range(2):
@@ -272,11 +274,13 @@
         same = query_seg == key_seg
         for h in range(heads_here):
             head = g * heads_here + h
-            line = jnp.broadcast_to(bias_line[head : head + 1, :], (rows, padded_length))
+            line = jnp.broadcast_to(bias_line[head : head + 1, :], (8, padded_length))
             skewed = pltpu.roll(line, padded_length - (rows - 1), 1, stride=1, stride_axis=0)
-            bias[g, h * rows : (h + 1) * rows, :] = jnp.where(
-                same, skewed[:, :window], masked_score
-            )
+            for first in range(0, rows, 8):
+                block = skewed if first == 0 else pltpu.roll(skewed, first, 1)
+                bias[g, h * rows + first : h * rows + first + 8, :] = jnp.where(
+                    same[first : first + 8], block[:, :window], masked_score
+                )
 
     head_of_lane = lax.broadcasted_iota(jnp.int32, (rows, CHUNK), 1) // head_width
 
@@ -287,7 +291,8 @@
 
         @pl.when(c_gets)
         def _():
-            c_copy(g, c_slot).wait_recv()
+            for part in range(2):
+                c_copy(g, part, c_slot).wait_recv()
 
         chunk_query = query[:, g * CHUNK : (g + 1) * CHUNK]
         stacked = jnp.concatenate(
@@ -308,27 +313,34 @@
             weights.astype(jnp.bfloat16), values_and_ones, preferred_element_type=jnp.float32
         )
         normal = (weighted[:, :CHUNK] / weighted[:, CHUNK:]).astype(jnp.bfloat16)
-        result = normal[0:rows]
+        chosen = normal[0:rows]
         for h in range(1, heads_here):
-            result = jnp.where(head_of_lane == h, normal[h * rows : (h + 1) * rows], result)
-        attended[:, g * CHUNK : (g + 1) * CHUNK] = result
-
-    def pass_z(g):
-        @pl.when(z_gets)
-        def _():
-            relay(g, y_slot, z_slot, z_send, z_recv, z_to).wait_recv()
-
-        @pl.when(jnp.logical_and(z_gets, jnp.logical_not(outer)))
-        def _():
-            c_copy(g, c_target).start()
-
-    local[3].wait()
-    for g in range(chunks):
-        make_bias(g)
+            chosen = jnp.where(head_of_lane == h, normal[h * rows : (h + 1) * rows], chosen)
+        attended[:, g * CHUNK : (g + 1) * CHUNK] = chosen
+
+    def pass_y(g):
         for part in range(2):
             y_copy(g, part, y_slot).wait_recv()
-        pl.when(z_sends)(lambda g=g: z_copy(g).start())
-        pl.when(outer)(lambda g=g: c_copy(g, c_target).start())
+            pl.when(z_sends)(z_copy(g, part).start)
+            pl.when(outer)(c_copy(g, part, c_target).start)
+
+    def pass_z(g):
+        for part in range(2):
+
+            @pl.when(z_gets)
+            def _():
+                relay(g, part, y_slot, z_slot, z_send, z_recv, z_to).wait_recv()
+
+            @pl.when(jnp.logical_and(z_gets, jnp.logical_not(outer)))
+            def _():
+                c_copy(g, part, c_target).start()
+
+    local[3].wait()
+    make_bias(0)
+    for g in range(chunks):
+        if g + 1 < chunks:
+            make_bias(g + 1)
+        pass_y(g)
         if g >= 1:
             pass_z(g - 1)
         if g >= 2:
@@ -413,39 +425,66 @@
             None, i, cols, [t for t in range(KERNEL) if is_own(i, t)]
         )
 
-    for j in range(gate_chunks):
-        pl.when(has_next)(lambda j=j: to_prev(j).wait_recv())
-        pl.when(has_prev)(lambda j=j: to_next(j).wait_recv())
-    left = gated[0:HALO, :].astype(jnp.float32)
-    right = gated[HALO + rows : 2 * HALO + rows, :].astype(jnp.float32)
-    plain[0:HALO, :] = left
-    plain[HALO + rows : 2 * HALO + rows, :] = right
-    offset4[0 : HALO - 4, :] = left[4:HALO]
-    offset4[HALO - 4 + rows : 2 * HALO - 4 + rows, :] = right
-    for i, cols in tiles:
-        here = slice(i * CONV_ROWS, (i + 1) * CONV_ROWS)
-        conv[here, cols] = add_taps(
-            conv[here, cols], i, cols, [t for t in range(KERNEL) if not is_own(i, t)]
-        )
+    for c in range(width // CONV_COLS):
+        half = slice(c * CONV_COLS, (c + 1) * CONV_COLS)
+        for j in range(half.start // GATE_COLS, half.stop // GATE_COLS):
+            pl.when(has_next)(lambda j=j: to_prev(j).wait_recv())
+            pl.when(has_prev)(lambda j=j: to_next(j).wait_recv())
+        left = gated[0:HALO, half].astype(jnp.float32)
+        right = gated[HALO + rows : 2 * HALO + rows, half].astype(jnp.float32)
+        plain[0:HALO, half] = left
+        plain[HALO + rows : 2 * HALO + rows, half] = right
+        offset4[0 : HALO - 4, half] = left[4:HALO]
+        offset4[HALO - 4 + rows : 2 * HALO - 4 + rows, half] = right
+        for i in range(rows // CONV_ROWS):
+            here = slice(i * CONV_ROWS, (i + 1) * CONV_ROWS)
+            conv[here, half] = add_taps(
+                conv[here, half], i, half, [t for t in range(KERNEL) if not is_own(i, t)]
+            )
 
     local[9].wait()
     inner = layer_norm(conv[...], inner_gain[...])
     activated = (inner * jax.nn.sigmoid(inner)).astype(jnp.bfloat16)
     local[10].wait()
-    out[...] = (
-        frames[...].astype(jnp.float32)
-        + jnp.dot(activated, shrink[...], preferred_element_type=jnp.float32)
-    ).astype(jnp.bfloat16)
+    leaving = []
+    for j in range(gate_chunks):
+        cols = slice(j * GATE_COLS, (j + 1) * GATE_COLS)
+        result[:, cols] = (
+            frames[:, cols].astype(jnp.float32)
+            + jnp.dot(activated, shrink[:, cols], preferred_element_type=jnp.float32)
+        ).astype(jnp.bfloat16)
+        leaving.append(
+            pltpu.make_async_copy(result.at[:, cols], out.at[:, cols], out_sem.at[j])
+        )
+        leaving[j].start()
 
     for g in range(chunks):
         for part in range(2):
             y_copy(g, part, y_target).wait_send()
             p_copy(g, part, p_target).wait_send()
-        pl.when(z_sends)(lambda g=g: z_copy(g).wait_send())
-        pl.when(c_sends)(lambda g=g: c_copy(g, c_target).wait_send())
+            pl.when(z_sends)(z_copy(g, part).wait_send)
+            pl.when(c_sends)(c_copy(g, part, c_target).wait_send)
     for j in range(gate_chunks):
         pl.when(has_prev)(lambda j=j: to_prev(j).wait_send())
         pl.when(has_next)(lambda j=j: to_next(j).wait_send())
+    for copy in leaving:
+        copy.wait()
+
+
+def hand_over(source, target, sems):
+    part_rows = source.shape[0] // sems.shape[0]
+    copies = [
+        pltpu.make_async_copy(
+            source.at[pl.ds(i * part_rows, part_rows), :],
+            target.at[pl.ds(i * part_rows, part_rows), :],
+            sems.at[i],
+        )
+        for i in range(sems.shape[0])
+    ]
+    for copy in copies:
+        copy.start()
+    for copy in copies:
+        copy.wait()
 
 
 def on_device(
@@ -471,14 +510,13 @@
     heads_here = CHUNK // (att_width // bucket_bias.shape[1])
     wide_rows = rows + 2 * HALO
     bf16, f32 = jnp.bfloat16, jnp.float32
-    vmem = pl.BlockSpec(memory_space=pltpu.VMEM)
     anywhere = pl.BlockSpec(memory_space=pl.ANY)
     dma = pltpu.SemaphoreType.DMA
-    return pl.pallas_call(
+    block_out = pl.pallas_call(
         functools.partial(kernel, lax.axis_size("seq")),
         out_shape=jax.ShapeDtypeStruct((rows, width), bf16),
         in_specs=[anywhere] * 13,
-        out_specs=vmem,
+        out_specs=anywhere,
         scratch_shapes=[
             pltpu.SMEM(utterance_lengths.shape, jnp.int32),
             pltpu.VMEM(bucket_table.shape, jnp.int32),
@@ -499,18 +537,20 @@
             pltpu.VMEM((wide_rows, width), f32),
             pltpu.VMEM((wide_rows, width), f32),
             pltpu.VMEM((rows, width), f32),
+            pltpu.VMEM((rows, width), bf16),
             dma((11,)),
             dma((chunks, 2)),
             dma((chunks, 2)),
             dma((chunks, 2)),
             dma((chunks, 2)),
             dma((chunks, 2)),
-            dma((chunks,)),
-            dma((chunks,)),
-            dma((chunks,)),
-            dma((chunks,)),
+            dma((chunks, 2)),
+            dma((chunks, 2)),
+            dma((chunks, 2)),
+            dma((chunks, 2)),
             dma((2, gate_chunks)),
             dma((2, gate_chunks)),
+            dma((gate_chunks,)),
         ],
         compiler_params=pltpu.CompilerParams(
             collective_id=0, has_side_effects=True, vmem_limit_bytes=60 * 1024 * 1024
@@ -530,6 +570,14 @@
         depth_taps,
         shrink_weight,
     )
+    return pl.pallas_call(
+        hand_over,
+        out_shape=jax.ShapeDtypeStruct((rows, width), bf16),
+        in_specs=[anywhere],
+        out_specs=anywhere,
+        scratch_shapes=[dma((4,))],
+        compiler_params=pltpu.CompilerParams(vmem_limit_bytes=60 * 1024 * 1024),
+    )(block_out)
 
 
 def solution(mesh):

time: 27.7 us -> 34.3 us (1.24)
  Pallas kernels: 25.9 us -> 34.1 us
  local copies, waits for them, and re-layouts: 1.67 us -> 0 us
    pallas_call x0 -> x1, Pallas kernels: none -> 9.08 us  [on_device(): pl.pallas_call(hand_over, out_shape=jax.ShapeDtypeStruct((rows, width), b...]
    unnamed x1 -> x0, local copies, waits for them, and re-layouts: 1.67 us -> none
    pallas_call x1, Pallas kernels: 25.9 us -> 25.1 us  [on_device(): pl.pallas_call(functools.partial(kernel, lax.axis_size('seq')), out_shape...]
where the time goes in v3:
time: 34.3 us; the launch traced here: 34.2 us
  Pallas kernels  34.1 us (99%)
    pallas_call x1, Pallas kernels, on_device(): pl.pallas_call(functools.partial(kernel, lax.axis_size('seq')), out_shape...  25.1 us
    pallas_call x1, Pallas kernels, on_device(): pl.pallas_call(hand_over, out_shape=jax.ShapeDtypeStruct((rows, width), b...  9.08 us

profile of v3, /device:TPU:11, one launch (start us, length us, event | category | flops | bytes accessed | tf_op | source)
XLA Modules:
  0.0 34.2 jit_solution(13067212876337612397)
XLA Ops:
  0.0 25.1 %shard_map.127.source = bf16[128,1024]{1,0:T(8,128)(2,1)} custom-call(s32[16]{0:T(128)} %lengths_hbm.1, s32[767]{0:T(1024)} %table_hbm.1, f32[8,32]{1,0:T(8,128)} %bitcast.3, f32[1,1024]{1,0:T(1,128)} %bitcast.4, f32[1,1024]{1,0:T(1,128)} %bitcast.5, bf16[128,1024]{1,0:T(8,128)(2,1)} %frames_hbm.1, bf16[128,512]{1,0:T(8,128)(2,1)} %query_hbm.1, ...), custom_call_target="tpu_custom_call" | custom-call | tf_op jit(solution)/shard_map/pallas_call | solution.py:515
  25.1 9.1 %shard_map.128 = bf16[128,1024]{1,0:T(8,128)(2,1)} custom-call(bf16[128,1024]{1,0:T(8,128)(2,1)} %shard_map.127.source), custom_call_target="tpu_custom_call" | custom-call | tf_op jit(solution)/shard_map/pallas_call | solution.py:573

commit v4 on v3

--- a/solution.py
+++ b/solution.py
@@ -64,6 +64,7 @@
     offset4,
     conv,
     result,
+    weights,
     local_sem,
     own_sem,
     p_send,
@@ -201,11 +202,10 @@
     def c_copy(g, part, target):
         return relay(g, part, c_source, target, c_send, c_recv, partner)
 
-    for g in range(chunks):
-        for part in range(2):
-            y_copy(g, part, y_target).start()
-        for part in range(2):
-            p_copy(g, part, p_target).start()
+    pieces = [(g, part) for part in range(2) for g in range(chunks)]
+    for g, part in pieces:
+        y_copy(g, part, y_target).start()
+        p_copy(g, part, p_target).start()
     for copy in local[4:]:
         copy.start()
 
@@ -284,16 +284,12 @@
 
     head_of_lane = lax.broadcasted_iota(jnp.int32, (rows, CHUNK), 1) // head_width
 
-    def attend(g):
-        for part in range(2):
-            own[part * chunks + g].wait()
-            p_copy(g, part, p_slot).wait_recv()
-
-        @pl.when(c_gets)
-        def _():
-            for part in range(2):
-                c_copy(g, part, c_slot).wait_recv()
-
+    def arrive(g, part):
+        own[part * chunks + g].wait()
+        p_copy(g, part, p_slot).wait_recv()
+        pl.when(c_gets)(c_copy(g, part, c_slot).wait_recv)
+
+    def weigh(g):
         chunk_query = query[:, g * CHUNK : (g + 1) * CHUNK]
         stacked = jnp.concatenate(
             [
@@ -307,54 +303,60 @@
         )
         scores = scores * (head_width**-0.5) + bias[g]
         top = jnp.max(scores, axis=1, keepdims=True)
-        weights = jnp.exp(scores - top)
+        weights[g] = jnp.exp(scores - top).astype(jnp.bfloat16)
+
+    def attend(g):
         values_and_ones = jnp.concatenate([kv[g, 1], jnp.ones_like(kv[g, 1])], axis=1)
-        weighted = jnp.dot(
-            weights.astype(jnp.bfloat16), values_and_ones, preferred_element_type=jnp.float32
-        )
+        weighted = jnp.dot(weights[g], values_and_ones, preferred_element_type=jnp.float32)
         normal = (weighted[:, :CHUNK] / weighted[:, CHUNK:]).astype(jnp.bfloat16)
         chosen = normal[0:rows]
         for h in range(1, heads_here):
             chosen = jnp.where(head_of_lane == h, normal[h * rows : (h + 1) * rows], chosen)
         attended[:, g * CHUNK : (g + 1) * CHUNK] = chosen
 
-    def pass_y(g):
-        for part in range(2):
-            y_copy(g, part, y_slot).wait_recv()
-            pl.when(z_sends)(z_copy(g, part).start)
-            pl.when(outer)(c_copy(g, part, c_target).start)
-
-    def pass_z(g):
-        for part in range(2):
-
-            @pl.when(z_gets)
-            def _():
-                relay(g, part, y_slot, z_slot, z_send, z_recv, z_to).wait_recv()
-
-            @pl.when(jnp.logical_and(z_gets, jnp.logical_not(outer)))
-            def _():
-                c_copy(g, part, c_target).start()
+    def use(g, part):
+        arrive(g, part)
+        (weigh, attend)[part](g)
+
+    def pass_y(g, part):
+        y_copy(g, part, y_slot).wait_recv()
+        pl.when(z_sends)(z_copy(g, part).start)
+        pl.when(outer)(c_copy(g, part, c_target).start)
+
+    def pass_z(g, part):
+        @pl.when(z_gets)
+        def _():
+            relay(g, part, y_slot, z_slot, z_send, z_recv, z_to).wait_recv()
+
+        @pl.when(jnp.logical_and(z_gets, jnp.logical_not(outer)))
+        def _():
+            c_copy(g, part, c_target).start()
+
+    half_att = att_width // 2
+
+    def project(half):
+        part = slice(half * half_att, (half + 1) * half_att)
+        return jnp.dot(attended[:, part], out_w[part, :], preferred_element_type=jnp.float32)
 
     local[3].wait()
     make_bias(0)
-    for g in range(chunks):
-        if g + 1 < chunks:
-            make_bias(g + 1)
-        pass_y(g)
-        if g >= 1:
-            pass_z(g - 1)
-        if g >= 2:
-            attend(g - 2)
-    pass_z(chunks - 1)
-    for g in range(max(0, chunks - 2), chunks):
-        attend(g)
-
+    make_bias(1)
+    for step, (g, part) in enumerate(pieces):
+        pass_y(g, part)
+        if step >= 1:
+            pass_z(*pieces[step - 1])
+        if part == 0 and g + 2 < chunks:
+            make_bias(g + 2)
+        if step >= 2:
+            use(*pieces[step - 2])
+    use(*pieces[-2])
     for copy in local[4:7]:
         copy.wait()
-    mid = (
-        frames[...].astype(jnp.float32)
-        + jnp.dot(attended[...], out_w[...], preferred_element_type=jnp.float32)
-    ).astype(jnp.bfloat16)
+    conv[...] = frames[...].astype(jnp.float32) + project(0)
+    pass_z(*pieces[-1])
+    use(*pieces[-1])
+
+    mid = (conv[...] + project(1)).astype(jnp.bfloat16)
     frames[...] = mid
     normed = layer_norm(mid.astype(jnp.float32), norm_gain[...]).astype(jnp.bfloat16)
     local[7].wait()
@@ -471,19 +473,24 @@
         copy.wait()
 
 
-def hand_over(source, target, sems):
-    part_rows = source.shape[0] // sems.shape[0]
-    copies = [
-        pltpu.make_async_copy(
-            source.at[pl.ds(i * part_rows, part_rows), :],
-            target.at[pl.ds(i * part_rows, part_rows), :],
-            sems.at[i],
-        )
-        for i in range(sems.shape[0])
+def hand_over(source, target, held, in_sems, out_sems):
+    count = in_sems.shape[0]
+    part_rows = source.shape[0] // count
+    parts = [pl.ds(i * part_rows, part_rows) for i in range(count)]
+    inward = [
+        pltpu.make_async_copy(source.at[part, :], held.at[part, :], in_sems.at[i])
+        for i, part in enumerate(parts)
     ]
-    for copy in copies:
+    outward = [
+        pltpu.make_async_copy(held.at[part, :], target.at[part, :], out_sems.at[i])
+        for i, part in enumerate(parts)
+    ]
+    for copy in inward:
         copy.start()
-    for copy in copies:
+    for first, second in zip(inward, outward):
+        first.wait()
+        second.start()
+    for copy in outward:
         copy.wait()
 
 
@@ -538,6 +545,7 @@
             pltpu.VMEM((wide_rows, width), f32),
             pltpu.VMEM((rows, width), f32),
             pltpu.VMEM((rows, width), bf16),
+            pltpu.VMEM((chunks, heads_here * rows, window), bf16),
             dma((11,)),
             dma((chunks, 2)),
             dma((chunks, 2)),
@@ -575,7 +583,7 @@
         out_shape=jax.ShapeDtypeStruct((rows, width), bf16),
         in_specs=[anywhere],
         out_specs=anywhere,
-        scratch_shapes=[dma((4,))],
+        scratch_shapes=[pltpu.VMEM((rows, width), bf16), dma((4,)), dma((4,))],
         compiler_params=pltpu.CompilerParams(vmem_limit_bytes=60 * 1024 * 1024),
     )(block_out)
 

time: 34.3 us -> 29.5 us (0.86)
  the two profiles are of different devices: /device:TPU:11 before, /device:TPU:1 now
where the time goes in v4:
time: 29.5 us; the launch traced here: 29.3 us
  Pallas kernels  29.3 us (99%)
    pallas_call x1, Pallas kernels, on_device(): pl.pallas_call(functools.partial(kernel, lax.axis_size('seq')), out_shape...  27.7 us
    pallas_call x1, Pallas kernels, on_device(): pl.pallas_call(hand_over, out_shape=jax.ShapeDtypeStruct((rows, width), b...  1.63 us

profile of v4, /device:TPU:1, one launch (start us, length us, event | category | flops | bytes accessed | tf_op | source)
XLA Modules:
  0.0 29.3 jit_solution(12038924444236050067)
XLA Ops:
  0.0 27.7 %shard_map.127.source = bf16[128,1024]{1,0:T(8,128)(2,1)} custom-call(s32[16]{0:T(128)} %lengths_hbm.1, s32[767]{0:T(1024)} %table_hbm.1, f32[8,32]{1,0:T(8,128)} %bitcast.3, f32[1,1024]{1,0:T(1,128)} %bitcast.4, f32[1,1024]{1,0:T(1,128)} %bitcast.5, bf16[128,1024]{1,0:T(8,128)(2,1)} %frames_hbm.1, bf16[128,512]{1,0:T(8,128)(2,1)} %query_hbm.1, ...), custom_call_target="tpu_custom_call" | custom-call | tf_op jit(solution)/shard_map/pallas_call | solution.py:522
  27.7 1.6 %shard_map.128 = bf16[128,1024]{1,0:T(8,128)(2,1)} custom-call(bf16[128,1024]{1,0:T(8,128)(2,1)} %shard_map.127.source), custom_call_target="tpu_custom_call" | custom-call | tf_op jit(solution)/shard_map/pallas_call | solution.py:581

commit v5 on v4

--- a/solution.py
+++ b/solution.py
@@ -14,6 +14,7 @@
 CHUNK = 128
 GATE_COLS = 256
 HALO = 64
+IN_FLIGHT = 3
 CONV_ROWS = 32
 CONV_COLS = 512
 
@@ -203,11 +204,13 @@
         return relay(g, part, c_source, target, c_send, c_recv, partner)
 
     pieces = [(g, part) for part in range(2) for g in range(chunks)]
-    for g, part in pieces:
+
+    def send_own(g, part):
         y_copy(g, part, y_target).start()
         p_copy(g, part, p_target).start()
-    for copy in local[4:]:
-        copy.start()
+
+    for piece in pieces[:IN_FLIGHT]:
+        send_own(*piece)
 
     @pl.when(jnp.logical_not(z_gets))
     def _():
@@ -343,6 +346,10 @@
     make_bias(1)
     for step, (g, part) in enumerate(pieces):
         pass_y(g, part)
+        if step + IN_FLIGHT < len(pieces):
+            send_own(*pieces[step + IN_FLIGHT])
+        for copy in local[4 + step : 5 + step]:
+            copy.start()
         if step >= 1:
             pass_z(*pieces[step - 1])
         if part == 0 and g + 2 < chunks:

time: 29.5 us -> 29.9 us (1.014)
  the two profiles are of different devices: /device:TPU:1 before, /device:TPU:11 now
where the time goes in v5:
time: 29.9 us; the launch traced here: 29.8 us
  Pallas kernels  29.7 us (99%)
    pallas_call x1, Pallas kernels, on_device(): pl.pallas_call(functools.partial(kernel, lax.axis_size('seq')), out_shape...  28.1 us
    pallas_call x1, Pallas kernels, on_device(): pl.pallas_call(hand_over, out_shape=jax.ShapeDtypeStruct((rows, width), b...  1.63 us

profile of v5, /device:TPU:11, one launch (start us, length us, event | category | flops | bytes accessed | tf_op | source)
XLA Modules:
  0.0 29.8 jit_solution(7915128897295312463)
XLA Ops:
  0.0 28.1 %shard_map.127.source = bf16[128,1024]{1,0:T(8,128)(2,1)} custom-call(s32[16]{0:T(128)} %lengths_hbm.1, s32[767]{0:T(1024)} %table_hbm.1, f32[8,32]{1,0:T(8,128)} %bitcast.3, f32[1,1024]{1,0:T(1,128)} %bitcast.4, f32[1,1024]{1,0:T(1,128)} %bitcast.5, bf16[128,1024]{1,0:T(8,128)(2,1)} %frames_hbm.1, bf16[128,512]{1,0:T(8,128)(2,1)} %query_hbm.1, ...), custom_call_target="tpu_custom_call" | custom-call | tf_op jit(solution)/shard_map/pallas_call | solution.py:529
  28.1 1.6 %shard_map.128 = bf16[128,1024]{1,0:T(8,128)(2,1)} custom-call(bf16[128,1024]{1,0:T(8,128)(2,1)} %shard_map.127.source), custom_call_target="tpu_custom_call" | custom-call | tf_op jit(solution)/shard_map/pallas_call | solution.py:588

commit v6 on v5

--- a/solution.py
+++ b/solution.py
@@ -14,7 +14,8 @@
 CHUNK = 128
 GATE_COLS = 256
 HALO = 64
-IN_FLIGHT = 3
+Z_LAG = 3
+USE_LAG = 5
 CONV_ROWS = 32
 CONV_COLS = 512
 
@@ -209,7 +210,7 @@
         y_copy(g, part, y_target).start()
         p_copy(g, part, p_target).start()
 
-    for piece in pieces[:IN_FLIGHT]:
+    for piece in pieces:
         send_own(*piece)
 
     @pl.when(jnp.logical_not(z_gets))
@@ -344,24 +345,22 @@
     local[3].wait()
     make_bias(0)
     make_bias(1)
-    for step, (g, part) in enumerate(pieces):
-        pass_y(g, part)
-        if step + IN_FLIGHT < len(pieces):
-            send_own(*pieces[step + IN_FLIGHT])
+    count_of = len(pieces)
+    for step in range(count_of + USE_LAG):
+        if step < count_of:
+            pass_y(*pieces[step])
         for copy in local[4 + step : 5 + step]:
             copy.start()
-        if step >= 1:
-            pass_z(*pieces[step - 1])
-        if part == 0 and g + 2 < chunks:
-            make_bias(g + 2)
-        if step >= 2:
-            use(*pieces[step - 2])
-    use(*pieces[-2])
-    for copy in local[4:7]:
-        copy.wait()
-    conv[...] = frames[...].astype(jnp.float32) + project(0)
-    pass_z(*pieces[-1])
-    use(*pieces[-1])
+        if 0 <= step - Z_LAG < count_of:
+            pass_z(*pieces[step - Z_LAG])
+        if step + 2 < chunks:
+            make_bias(step + 2)
+        if step == count_of + USE_LAG - 1:
+            for copy in local[4:7]:
+                copy.wait()
+            conv[...] = frames[...].astype(jnp.float32) + project(0)
+        if step >= USE_LAG:
+            use(*pieces[step - USE_LAG])
 
     mid = (conv[...] + project(1)).astype(jnp.bfloat16)
     frames[...] = mid

time: 29.9 us -> 26.1 us (0.87)
  Pallas kernels: 29.7 us -> 25.9 us
    pallas_call x1, Pallas kernels: 28.1 us -> 24.3 us  [on_device(): pl.pallas_call(functools.partial(kernel, lax.axis_size('seq')), out_shape...]
where the time goes in v6:
time: 26.1 us; the launch traced here: 25.9 us
  Pallas kernels  25.9 us (99%)
    pallas_call x1, Pallas kernels, on_device(): pl.pallas_call(functools.partial(kernel, lax.axis_size('seq')), out_shape...  24.3 us
    pallas_call x1, Pallas kernels, on_device(): pl.pallas_call(hand_over, out_shape=jax.ShapeDtypeStruct((rows, width), b...  1.63 us

profile of v6, /device:TPU:11, one launch (start us, length us, event | category | flops | bytes accessed | tf_op | source)
XLA Modules:
  0.0 25.9 jit_solution(18272123877887705181)
XLA Ops:
  0.0 24.3 %shard_map.127.source = bf16[128,1024]{1,0:T(8,128)(2,1)} custom-call(s32[16]{0:T(128)} %lengths_hbm.1, s32[767]{0:T(1024)} %table_hbm.1, f32[8,32]{1,0:T(8,128)} %bitcast.3, f32[1,1024]{1,0:T(1,128)} %bitcast.4, f32[1,1024]{1,0:T(1,128)} %bitcast.5, bf16[128,1024]{1,0:T(8,128)(2,1)} %frames_hbm.1, bf16[128,512]{1,0:T(8,128)(2,1)} %query_hbm.1, ...), custom_call_target="tpu_custom_call" | custom-call | tf_op jit(solution)/shard_map/pallas_call | solution.py:528
  24.3 1.6 %shard_map.128 = bf16[128,1024]{1,0:T(8,128)(2,1)} custom-call(bf16[128,1024]{1,0:T(8,128)(2,1)} %shard_map.127.source), custom_call_target="tpu_custom_call" | custom-call | tf_op jit(solution)/shard_map/pallas_call | solution.py:587

commit v7 on v6

--- a/solution.py
+++ b/solution.py
@@ -14,8 +14,8 @@
 CHUNK = 128
 GATE_COLS = 256
 HALO = 64
-Z_LAG = 3
-USE_LAG = 5
+Z_LAG = 4
+USE_LAG = 7
 CONV_ROWS = 32
 CONV_COLS = 512
 
@@ -400,8 +400,9 @@
         )
         units = (linear * jax.nn.sigmoid(gate)).astype(jnp.bfloat16)
         gated[HALO : HALO + rows, cols] = units
-        pl.when(has_prev)(lambda j=j: to_prev(j).start())
-        pl.when(has_next)(lambda j=j: to_next(j).start())
+        pl.when(jnp.logical_and(has_next, core == 1))(to_next(j).start)
+        pl.when(has_prev)(to_prev(j).start)
+        pl.when(jnp.logical_and(has_next, core == 0))(to_next(j).start)
         wide = units.astype(jnp.float32)
         plain[HALO : HALO + rows, cols] = wide
         offset4[HALO - 4 : HALO - 4 + rows, cols] = wide

time: 26.1 us -> 25.1 us (0.962); the launches traced: 25.9 us -> 24.6 us
  Pallas kernels: 25.9 us -> 24.6 us
    pallas_call x1, Pallas kernels: 24.3 us -> 23 us  [on_device(): pl.pallas_call(functools.partial(kernel, lax.axis_size('seq')), out_shape...]
where the time goes in v7:
time: 25.1 us; the launch traced here: 24.6 us
  Pallas kernels  24.6 us (98%)
    pallas_call x1, Pallas kernels, on_device(): pl.pallas_call(functools.partial(kernel, lax.axis_size('seq')), out_shape...  23 us
    pallas_call x1, Pallas kernels, on_device(): pl.pallas_call(hand_over, out_shape=jax.ShapeDtypeStruct((rows, width), b...  1.63 us

profile of v7, /device:TPU:11, one launch (start us, length us, event | category | flops | bytes accessed | tf_op | source)
XLA Modules:
  0.0 24.6 jit_solution(1007443432169614248)
XLA Ops:
  0.0 23.0 %shard_map.127.source = bf16[128,1024]{1,0:T(8,128)(2,1)} custom-call(s32[16]{0:T(128)} %lengths_hbm.1, s32[767]{0:T(1024)} %table_hbm.1, f32[8,32]{1,0:T(8,128)} %bitcast.3, f32[1,1024]{1,0:T(1,128)} %bitcast.4, f32[1,1024]{1,0:T(1,128)} %bitcast.5, bf16[128,1024]{1,0:T(8,128)(2,1)} %frames_hbm.1, bf16[128,512]{1,0:T(8,128)(2,1)} %query_hbm.1, ...), custom_call_target="tpu_custom_call" | custom-call | tf_op jit(solution)/shard_map/pallas_call | solution.py:529
  23.0 1.6 %shard_map.128 = bf16[128,1024]{1,0:T(8,128)(2,1)} custom-call(bf16[128,1024]{1,0:T(8,128)(2,1)} %shard_map.127.source), custom_call_target="tpu_custom_call" | custom-call | tf_op jit(solution)/shard_map/pallas_call | solution.py:588

commit v8 on v7

--- a/solution.py
+++ b/solution.py
@@ -205,13 +205,8 @@
         return relay(g, part, c_source, target, c_send, c_recv, partner)
 
     pieces = [(g, part) for part in range(2) for g in range(chunks)]
-
-    def send_own(g, part):
+    for g, part in pieces:
         y_copy(g, part, y_target).start()
-        p_copy(g, part, p_target).start()
-
-    for piece in pieces:
-        send_own(*piece)
 
     @pl.when(jnp.logical_not(z_gets))
     def _():
@@ -349,6 +344,7 @@
     for step in range(count_of + USE_LAG):
         if step < count_of:
             pass_y(*pieces[step])
+            p_copy(*pieces[step], p_target).start()
         for copy in local[4 + step : 5 + step]:
             copy.start()
         if 0 <= step - Z_LAG < count_of:

time: 25.1 us -> 25.1 us (level)
  no operation moved by 1% of the time
where the time goes in v8:
time: 25.1 us; the launch traced here: 24.6 us
  Pallas kernels  24.6 us (98%)
    pallas_call x1, Pallas kernels, on_device(): pl.pallas_call(functools.partial(kernel, lax.axis_size('seq')), out_shape...  23 us
    pallas_call x1, Pallas kernels, on_device(): pl.pallas_call(hand_over, out_shape=jax.ShapeDtypeStruct((rows, width), b...  1.63 us

profile of v8, /device:TPU:11, one launch (start us, length us, event | category | flops | bytes accessed | tf_op | source)
XLA Modules:
  0.0 24.6 jit_solution(2769854101465882524)
XLA Ops:
  0.0 23.0 %shard_map.127.source = bf16[128,1024]{1,0:T(8,128)(2,1)} custom-call(s32[16]{0:T(128)} %lengths_hbm.1, s32[767]{0:T(1024)} %table_hbm.1, f32[8,32]{1,0:T(8,128)} %bitcast.3, f32[1,1024]{1,0:T(1,128)} %bitcast.4, f32[1,1024]{1,0:T(1,128)} %bitcast.5, bf16[128,1024]{1,0:T(8,128)(2,1)} %frames_hbm.1, bf16[128,512]{1,0:T(8,128)(2,1)} %query_hbm.1, ...), custom_call_target="tpu_custom_call" | custom-call | tf_op jit(solution)/shard_map/pallas_call | solution.py:525
  23.0 1.6 %shard_map.128 = bf16[128,1024]{1,0:T(8,128)(2,1)} custom-call(bf16[128,1024]{1,0:T(8,128)(2,1)} %shard_map.127.source), custom_call_target="tpu_custom_call" | custom-call | tf_op jit(solution)/shard_map/pallas_call | solution.py:584

commit v9 on v7

--- a/solution.py
+++ b/solution.py
@@ -15,7 +15,7 @@
 GATE_COLS = 256
 HALO = 64
 Z_LAG = 4
-USE_LAG = 7
+USE_LAG = 6
 CONV_ROWS = 32
 CONV_COLS = 512
 

time: 25.1 us -> 25.2 us (level); the launches traced: 24.6 us -> 25 us
  Pallas kernels: 24.6 us -> 25 us
    pallas_call x1, Pallas kernels: 23 us -> 23.4 us  [on_device(): pl.pallas_call(functools.partial(kernel, lax.axis_size('seq')), out_shape...]
where the time goes in v9:
time: 25.2 us; the launch traced here: 25 us
  Pallas kernels  25 us (99%)
    pallas_call x1, Pallas kernels, on_device(): pl.pallas_call(functools.partial(kernel, lax.axis_size('seq')), out_shape...  23.4 us
    pallas_call x1, Pallas kernels, on_device(): pl.pallas_call(hand_over, out_shape=jax.ShapeDtypeStruct((rows, width), b...  1.63 us

profile of v9, /device:TPU:11, one launch (start us, length us, event | category | flops | bytes accessed | tf_op | source)
XLA Modules:
  0.0 25.0 jit_solution(6924083218069533525)
XLA Ops:
  0.0 23.4 %shard_map.127.source = bf16[128,1024]{1,0:T(8,128)(2,1)} custom-call(s32[16]{0:T(128)} %lengths_hbm.1, s32[767]{0:T(1024)} %table_hbm.1, f32[8,32]{1,0:T(8,128)} %bitcast.3, f32[1,1024]{1,0:T(1,128)} %bitcast.4, f32[1,1024]{1,0:T(1,128)} %bitcast.5, bf16[128,1024]{1,0:T(8,128)(2,1)} %frames_hbm.1, bf16[128,512]{1,0:T(8,128)(2,1)} %query_hbm.1, ...), custom_call_target="tpu_custom_call" | custom-call | tf_op jit(solution)/shard_map/pallas_call | solution.py:529
  23.4 1.6 %shard_map.128 = bf16[128,1024]{1,0:T(8,128)(2,1)} custom-call(bf16[128,1024]{1,0:T(8,128)(2,1)} %shard_map.127.source), custom_call_target="tpu_custom_call" | custom-call | tf_op jit(solution)/shard_map/pallas_call | solution.py:588
